TPU v7x, 32 devices: a whole 2x2x4 slice. The times are simulated.
32 devices in a mesh: parts: 2 (over y), rep: 4 (over x, core), tp: 4 (over z).
Axes of the slice: x: 2, y: 2, z: 4, core: 2. Of those that a mesh axis runs over, the one named last changes fastest.
Arguments:
- queries: bfloat16 [1024, 8, 128], P(('parts', 'rep'), 'tp'), parts along dimension 0, may hold values from -120 to 120
- fresh_kv: bfloat16 [1024, 8, 2, 128], P(('parts', 'rep'), 'tp'), parts along dimension 0, may hold values from -6 to 6, as said below
- kv_pool: bfloat16 [8960, 8, 2, 16, 128], P(('parts', 'rep'), 'tp'), parts along dimension 0, may hold values from -6 to 6, as said below
- page_table: int32 [1024, 8], P(('parts', 'rep')), parts along dimension 0, may hold values from 0 to 1119, as said below
- lengths: int32 [1024], P(('parts', 'rep')), parts along dimension 0, may hold values from 2 to 128
- mig_src: int32 [8, 4, 32], P(('parts', 'rep')), parts along dimension 0, may hold values from 0 to 1118, as said below
- mig_dst: int32 [8, 4, 32], P(('parts', 'rep')), parts along dimension 0, may hold values from 0 to 1119, as said below
- mig_count: int32 [8, 4], P(('parts', 'rep')), parts along dimension 0, may hold values from 0 to 32, as said below
- residual: bfloat16 [1024, 12288], P(('parts', 'rep'), 'tp'), parts along dimension 0, may hold values from -11 to 11
- out_weight: bfloat16 [1024, 12288], P('tp'), may hold values from -0.5 to 0.5
- norm_gain: bfloat16 [12288], replicated, may hold values from 0.5 to 1.5
Outputs:
- layer_out: bfloat16 [1024, 12288], P(('parts', 'rep'), 'tp'), parts along dimension 0
There are 2 independent parts, one for each index of `parts`. A program takes and returns all parts, laid end to end along the dimension named above; an argument that names none is the same for every part. Nothing has to cross between parts.
Inputs may be any that keep to these rules, and one draw needn't show every extreme that they name: `page_table`: the 8 entries of a row are distinct pages of its replica's pool; rows of one replica share no page. `mig_src`: entries j >= mig_count[d, s] are unused; used entries of one source are distinct pages that no row of its page_table names. `mig_dst`: used entries of one destination are distinct and are pages that its page_table names, whole requests' pages at a time; entries j >= mig_count[d, s] are unused. `mig_count`: A multiple of 8; zero when d equals s. `fresh_kv`: copies c and c2 hold equal numbers when c * 1 equals c2 * 1. `kv_pool`: copies c and c2 hold equal numbers when c * 1 equals c2 * 1.
All inputs are finite; a program needn't handle non-finite values.
Results may differ from a plain program's by a relative error of at most 0.0054.
Values may be sent and summed in bfloat16 or wider, within the bound.
A program may use at most 192 MiB of HBM per device.

v0:
```python
import jax
import jax.numpy as jnp
from jax import lax
from jax.sharding import PartitionSpec as P

EPSILON = 1e-05


def on_device(
    queries,
    fresh_kv,
    kv_pool,
    page_table,
    lengths,
    mig_src,
    mig_dst,
    mig_count,
    residual,
    out_weight,
    norm_gain,
):
    tp_ranks = lax.axis_size("tp")
    slot_count, head_count, head_width = queries.shape
    copy_count = kv_pool.shape[1]
    group_size = head_count // copy_count
    pool_pages = kv_pool.shape[0]
    capacity = mig_src.shape[2]
    block_shape = kv_pool.shape[1:]
    outgoing = kv_pool[mig_src[0].reshape(-1)].reshape((mig_src.shape[1], capacity) + block_shape)
    incoming = lax.all_to_all(outgoing, "rep", split_axis=0, concat_axis=0, tiled=True)
    arrived = jnp.arange(capacity, dtype=jnp.int32)[None, :] < mig_count[0][:, None]
    targets = jnp.where(arrived, mig_dst[0], pool_pages).reshape(-1)
    moved_pool = kv_pool.at[targets].set(incoming.reshape((-1,) + block_shape), mode="drop")
    page_blocks = moved_pool[page_table]
    page_count = page_blocks.shape[1]
    page_size = page_blocks.shape[4]
    token_span = page_count * page_size
    key_blocks = page_blocks[:, :, :, 0]
    value_blocks = page_blocks[:, :, :, 1]
    query_groups = queries.reshape(slot_count, copy_count, group_size, head_width)
    scaling = head_width ** (-0.5)
    scores = jnp.einsum(
        "scgd,smcpd->scgmp", query_groups, key_blocks, preferred_element_type=jnp.float32
    )
    scores = scores.reshape(slot_count, copy_count, group_size, token_span) * scaling
    self_score = (
        jnp.einsum(
            "scgd,scd->scg", query_groups, fresh_kv[:, :, 0], preferred_element_type=jnp.float32
        )
        * scaling
    )
    live_mask = jnp.arange(token_span, dtype=jnp.int32)[None, :] < lengths[:, None]
    scores = jnp.where(live_mask[:, None, None, :], scores, -jnp.inf)
    highest = jnp.maximum(jnp.max(scores, axis=3), self_score)
    cache_mass = jnp.exp(scores - highest[..., None])
    self_mass = jnp.exp(self_score - highest)
    total_mass = jnp.sum(cache_mass, axis=3) + self_mass
    weights = (cache_mass / total_mass[..., None]).astype(jnp.bfloat16)
    self_weight = (self_mass / total_mass).astype(jnp.bfloat16)
    weights = weights.reshape(slot_count, copy_count, group_size, page_count, page_size)
    context = jnp.einsum(
        "scgmp,smcpd->scgd", weights, value_blocks, preferred_element_type=jnp.float32
    )
    context = (
        context
        + self_weight.astype(jnp.float32)[..., None]
        * fresh_kv[:, :, 1].astype(jnp.float32)[:, :, None, :]
    )
    attended = context.reshape(slot_count, head_count * head_width).astype(jnp.bfloat16)
    model_width = out_weight.shape[1]
    local_width = model_width // tp_ranks
    feature_share = lax.psum_scatter(
        lax.dot_general(
            out_weight, attended, (((0,), (1,)), ((), ())), preferred_element_type=jnp.float32
        ),
        "tp",
        scatter_dimension=0,
        tiled=True,
    )
    mixed_out = feature_share.T + residual.astype(jnp.float32)
    squares = lax.psum(jnp.sum(mixed_out * mixed_out, axis=1), "tp")
    scaled = mixed_out * lax.rsqrt(squares / model_width + EPSILON)[:, None]
    local_gain = lax.dynamic_slice_in_dim(
        norm_gain, lax.axis_index("tp") * local_width, local_width, 0
    )
    return (local_gain.astype(jnp.float32)[None, :] * scaled).astype(jnp.bfloat16)


def solution(mesh):
    in_specs = (
        P(("parts", "rep"), "tp", None),
        P(("parts", "rep"), "tp", None, None),
        P(("parts", "rep"), "tp", None, None, None),
        P(("parts", "rep"), None),
        P(("parts", "rep")),
        P(("parts", "rep"), None, None),
        P(("parts", "rep"), None, None),
        P(("parts", "rep"), None),
        P(("parts", "rep"), "tp"),
        P("tp", None),
        P(),
    )
    out_specs = P(("parts", "rep"), "tp")
    return jax.shard_map(
        on_device, mesh=mesh, in_specs=in_specs, out_specs=out_specs, check_vma=False
    )
```

profile of v0, /device:TPU:0, one launch (start us, length us, event | category | flops | bytes accessed | tf_op | source)
XLA Modules:
  0.0 276.7 jit_solution(7419850057774387295)
XLA Ops:
  6.5 0.0 copy-start.4
  6.5 17.3 %copy.45 = bf16[1120,2,2,16,128]{4,3,2,1,0:T(8,128)(2,1)} copy(bf16[1120,2,2,16,128]{4,3,2,1,0:T(8,128)(2,1)} %param.13) | data formatting | bytes 36700160
  23.8 0.0 copy-done.4
  23.8 0.0 copy-start.7
  23.8 0.0 copy-start.3
  23.9 0.0 copy-start.2
  23.9 0.0 copy-start.1
  23.9 0.0 copy-start.6
  23.9 0.1 reshape_squeeze.3
  24.0 8.3 %gather_fusion = bf16[128,2,2,16,128]{4,3,2,1,0:T(8,128)(2,1)} fusion(bf16[1120,2,2,16,128]{4,3,2,1,0:T(8,128)(2,1)} %copy.45, s32[1024]{0:T(1024)S(1)} %pad_clamp_fusion), kind=kCustom, calls=%fused_computation | custom fusion | bytes 4194816 | tf_op jit(solution)/shard_map/gather | solution.py:29
  32.3 4.2 %all-to-all-start = ((bf16[4,32,2,2,16,128]{5,4,3,2,1,0:T(8,128)(2,1)}), bf16[4,32,2,2,16,128]{5,4,3,2,1,0:T(8,128)(2,1)S(1)}, u32[]{:S(2)}, u32[]{:S(2)}) async-start(bf16[4,32,2,2,16,128]{5,4,3,2,1,0:T(8,128)(2,1)} %bitcast.51), calls=%async_computation | async-start | bytes 4194304 | tf_op jit(solution)/shard_map/all_to_all | solution.py:30
  36.5 0.0 reduce-scatter.2.cloned.1.call-start
  36.5 0.0 copy-done.7
  36.5 0.1 iota_compare_fusion
  36.6 0.1 lt.95
  36.7 0.0 copy-done.5
  36.7 0.1 squeeze.13
  36.8 0.0 copy-done.3
  36.8 0.1 copy.14
  36.9 0.1 reshape.172
  37.0 0.0 copy-done.2
  37.1 0.0 copy-done.1
  37.1 0.2 slice_convert_fusion
  37.3 0.1 multiply_reduce_fusion.1
  37.4 0.0 copy-done.6
  37.4 0.1 broadcast_compare_fusion
  37.5 24.7 %all-to-all-done = bf16[4,32,2,2,16,128]{5,4,3,2,1,0:T(8,128)(2,1)S(1)} async-done(((bf16[4,32,2,2,16,128]{5,4,3,2,1,0:T(8,128)(2,1)}), bf16[4,32,2,2,16,128]{5,4,3,2,1,0:T(8,128)(2,1)S(1)}, u32[]{:S(2)}, u32[]{:S(2)}) %all-to-all-start) | async-done | bytes 2097184 | tf_op jit(solution)/shard_map/all_to_all | solution.py:30
  62.2 16.9 %scatter_fusion = bf16[1120,2,2,16,128]{4,3,2,1,0:T(8,128)(2,1)} fusion(bf16[1120,2,2,16,128]{4,3,2,1,0:T(8,128)(2,1)} %copy.45, s32[128]{0:T(128)S(1)} %fusion.11, bf16[128,2,2,16,128]{4,3,2,1,0:T(8,128)(2,1)S(1)} %bitcast.50), kind=kCustom, calls=%fused_computation.2 | custom fusion | bytes 6291968 | tf_op jit(solution)/shard_map/scatter | solution.py:33
  79.1 19.7 %gather_fusion.1 = bf16[1024,2,2,16,128]{4,3,2,1,0:T(8,128)(2,1)} fusion(bf16[1120,2,2,16,128]{4,3,2,1,0:T(8,128)(2,1)} %scatter_fusion, s32[1024]{0:T(1024)S(1)} %broadcast_clamp_fusion), kind=kCustom, calls=%fused_computation.1 | custom fusion | bytes 33558528 | tf_op jit(solution)/shard_map/gather | solution.py:34
  98.8 11.3 %slice_bitcast_fusion = (bf16[128,8,2,16,128]{4,3,2,1,0:T(8,128)(2,1)}, bf16[128,8,2,16,128]{4,3,2,1,0:T(8,128)(2,1)S(1)}) fusion(bf16[128,8,2,2,16,128]{5,4,3,2,1,0:T(8,128)(2,1)} %bitcast.49), kind=kLoop, calls=%fused_computation.4 | loop fusion | bytes 33554432 | tf_op jit(solution)/shard_map/squeeze | solution.py:39
  110.2 19.5 %fusion.2 = f32[128,2,1,8,16]{4,2,3,1,0:T(1,128)S(1)} fusion(bf16[128,8,2,16,128]{4,3,2,1,0:T(8,128)(2,1)S(1)} %get-tuple-element.6, bf16[128,2,128,1,1]{2,1,0,3,4:T(2,128)(2,1)S(1)} %bitcast.57), kind=kOutput, calls=%fused_computation.8 | convolution fusion | flops 8388608 | bytes 8585216 | tf_op jit(solution)/shard_map/scgd,smcpd->scgmp/dot_general | solution.py:42
  129.7 0.6 copy.19
  130.3 0.0 slice-start
  130.4 0.1 fusion.6
  130.5 1.1 copy.24
  131.6 0.1 copy.16
  131.7 6.4 %fusion = f32[128,2,1,128,1]{3,2,4,1,0:T(1,128)S(1)} fusion(bf16[128,2,8,16,1]{3,4,2,1,0:T(2,128)(2,1)S(1)} %copy.24, bf16[128,8,2,16,128]{4,3,2,1,0:T(8,128)(2,1)} %get-tuple-element.5), kind=kOutput, calls=%fused_computation.6 | convolution fusion | flops 8388608 | bytes 8585216 | tf_op jit(solution)/shard_map/scgmp,smcpd->scgd/dot_general | solution.py:61
  138.1 0.2 add_convert_fusion
  138.3 0.0 slice-done
  138.4 0.0 slice-done.1
  138.4 3.6 %convolution_bitcast_fusion = f32[12288,128]{0,1:T(8,128)} fusion(bf16[256,12288]{1,0:T(8,128)(2,1)S(1)} %bitcast.53, bf16[16,8,2,128]{3,2,1,0:T(2,128)(2,1)S(1)} %bitcast.55), kind=kOutput, calls=%fused_computation.3 | convolution fusion | flops 805306368 | bytes 12648448 | tf_op jit(solution)/shard_map/dot_general | solution.py:73
  142.0 0.0 reduce-scatter.2.cloned.1.call-update
  142.1 0.8 dynamic-slice_convert_fusion
  142.8 111.8 %reduce-scatter.2.cloned.1.call-done = f32[3072,128]{0,1:T(8,128)} async-done(((f32[12288,128]{0,1:T(8,128)}), f32[3072,128]{0,1:T(8,128)}) %reduce-scatter.2.cloned.1.call-update) | async-done | bytes 1572880 | tf_op jit(solution)/shard_map/reduce_scatter | solution.py:72
  254.7 0.0 copy-done
  254.7 1.7 multiply_reduce_fusion
  256.4 10.9 %psum.7 = f32[128]{0:T(128)S(1)} all-reduce(f32[128]{0:T(128)S(1)} %multiply_reduce_fusion), channel_id=1, replica_groups=mesh['parts'=2,'rep'=4,'tp'=4] {'tp'}, use_global_device_ids=true, to_apply=%region_5.6 | all-reduce | flops 128 | bytes 1024 | tf_op jit(solution)/shard_map/psum | solution.py:81
  267.3 2.6 multiply_convert_fusion
  (16 shorter events, 0.2 us)
Async XLA Ops:
  6.5 17.3 %copy-start.4 = (s32[1,4,32]{2,1,0:T(4,128)S(1)}, s32[1,4,32]{2,1,0:T(4,128)}, u32[]{:S(2)}) copy-start(s32[1,4,32]{2,1,0:T(4,128)} %param.16) | copy-start | bytes 1540
  23.8 12.7 %copy-start.7 = (s32[1,4]{1,0:T(1,128)S(1)}, s32[1,4]{1,0:T(1,128)}, u32[]{:S(2)}) copy-start(s32[1,4]{1,0:T(1,128)} %param.18) | copy-start | bytes 52
  23.8 12.9 %copy-start.5 = (s32[1,4,32]{2,1,0:T(4,128)S(1)}, s32[1,4,32]{2,1,0:T(4,128)}, u32[]{:S(2)}) copy-start(s32[1,4,32]{2,1,0:T(4,128)} %param.17) | copy-start | bytes 1540
  23.8 13.0 %copy-start.3 = (s32[128,8]{0,1:T(8,128)S(1)}, s32[128,8]{0,1:T(8,128)}, u32[]{:S(2)}) copy-start(s32[128,8]{0,1:T(8,128)} %param.14) | copy-start | bytes 12292
  23.9 13.2 %copy-start.2 = (bf16[128,2,128]{2,1,0:T(2,128)(2,1)S(1)}, bf16[128,2,128]{2,1,0:T(2,128)(2,1)}, u32[]{:S(2)}) copy-start(bf16[128,2,128]{2,1,0:T(2,128)(2,1)} %param.11) | copy-start | bytes 196612
  23.9 13.2 %copy-start.1 = (bf16[128,2,2,128]{3,2,1,0:T(2,128)(2,1)S(1)}, bf16[128,2,2,128]{3,2,1,0:T(2,128)(2,1)}, u32[]{:S(2)}) copy-start(bf16[128,2,2,128]{3,2,1,0:T(2,128)(2,1)} %param.12) | copy-start | bytes 393220
  23.9 13.5 %copy-start.6 = (s32[128]{0:T(128)S(1)}, s32[128]{0:T(128)}, u32[]{:S(2)}) copy-start(s32[128]{0:T(128)} %param.15) | copy-start | bytes 1540
  32.3 29.9 %all-to-all-start = ((bf16[4,32,2,2,16,128]{5,4,3,2,1,0:T(8,128)(2,1)}), bf16[4,32,2,2,16,128]{5,4,3,2,1,0:T(8,128)(2,1)S(1)}, u32[]{:S(2)}, u32[]{:S(2)}) async-start(bf16[4,32,2,2,16,128]{5,4,3,2,1,0:T(8,128)(2,1)} %bitcast.51), calls=%async_computation | async-start | bytes 4194304 | tf_op jit(solution)/shard_map/all_to_all | solution.py:30
  36.5 218.1 %reduce-scatter.2.cloned.1.call-start = ((), (), s32[]{:S(2)}) async-start(), calls=%async_computation.2 | async-start | bytes 7864320 | tf_op jit(solution)/shard_map/reduce_scatter | solution.py:72
  130.3 8.0 %slice-start = ((s8[6291456]{0:T(1024)(128)(4,1)}), s8[2097152]{0:T(1024)(128)(4,1)S(1)}, s32[]{:S(2)}) async-start(s8[6291456]{0:T(1024)(128)(4,1)} %bitcast.52), calls=%async_computation.3 | async-start | bytes 4194304
  131.7 6.6 %slice-start.1 = ((s8[6291456]{0:T(1024)(128)(4,1)}), s8[4194304]{0:T(1024)(128)(4,1)S(1)}, s32[]{:S(2)}) async-start(s8[6291456]{0:T(1024)(128)(4,1)} %bitcast.52), calls=%async_computation.4 | async-start | bytes 8388608
  142.0 112.6 %copy-start = (bf16[128,3072]{1,0:T(8,128)(2,1)S(1)}, bf16[128,3072]{1,0:T(8,128)(2,1)}, u32[]{:S(2)}) copy-start(bf16[128,3072]{1,0:T(8,128)(2,1)} %param.19) | copy-start | bytes 2359300
Sparse Core Ops, SparseCore 0:
  142.2 112.4 reduce-scatter.1
where the time goes:
time: 278 us; the launch traced here: 277 us
  waiting for transfers between devices  137 us (49%)
  local copies, waits for them, and re-layouts  75.9 us (27%)
  matrix products  29.6 us (11%)
  between operations  13.6 us (5%)
  blocking collectives  10.9 us (4%)
  other arithmetic  5.93 us (2%)
  starting transfers between devices  4.21 us (2%)
    reduce_scatter x1, waiting for transfers between devices, on_device(): lax.psum_scatter(lax.dot_general(out_weight, attended, (((0,), (1,)), (()...  112 us
    all_to_all x1, waiting for transfers between devices, on_device(): lax.all_to_all(outgoing, 'rep', split_axis=0, concat_axis=0, tiled=True)  24.7 us
    gather x1, local copies, waits for them, and re-layouts, on_device(): page_blocks = moved_pool[page_table]  19.7 us
    dot_general x1, matrix products, on_device(): jnp.einsum('scgd,smcpd->scgmp', query_groups, key_blocks, preferred_eleme...  19.5 us
    unnamed x21, local copies, waits for them, and re-layouts  17.3 us
    scatter x1, local copies, waits for them, and re-layouts, on_device(): kv_pool.at[targets].set(incoming.reshape((-1,) + block_shape), mode='drop')  16.9 us
    squeeze x1, local copies, waits for them, and re-layouts, on_device(): value_blocks = page_blocks[:, :, :, 1]  11.3 us
    psum x1, blocking collectives, on_device(): squares = lax.psum(jnp.sum(mixed_out * mixed_out, axis=1), 'tp')  10.9 us
  transfers between devices with their start and end apart: 2, of which 2 were waited for; matrix products, arithmetic and copies ran while one was open for 1% of the time, Pallas kernels for 0%

commit v1 on v0

v1 whole, which is shorter than its diff:
```python
import functools
import math

import jax
import jax.numpy as jnp
import numpy as np
from jax import lax
from jax.experimental import pallas as pl
from jax.experimental.pallas import tpu as pltpu
from jax.sharding import PartitionSpec as P

EPSILON = 1e-05
NEVER = -1e30


def attend_kernel(
    rows, group, page_size, step_pages, factor,
    query_ref, fresh_ref, table_ref, code_ref, spread_ref, pool_ref, out_ref, top_ref, mass_ref, sum_ref,
):
    step = pl.program_id(0)
    copies = query_ref.shape[0]
    width = query_ref.shape[2]
    tokens = step_pages * page_size

    @pl.when(step == 0)
    def _():
        for c in range(copies):
            fresh_key = fresh_ref[c, 0].astype(jnp.float32)
            fresh_value = fresh_ref[c, 1].astype(jnp.float32)
            for g in range(group):
                part = slice(g * rows, (g + 1) * rows)
                own = jnp.sum(query_ref[c, part].astype(jnp.float32) * fresh_key, axis=1, keepdims=True)
                top_ref[c, part] = jnp.broadcast_to(own, (rows, width))
                mass_ref[c, part] = jnp.ones((rows, width), jnp.float32)
                sum_ref[c, part] = fresh_value

    page = lax.broadcasted_iota(jnp.int32, (rows, step_pages), 1) + step * step_pages
    found = jnp.zeros((rows, step_pages), jnp.float32)
    for m in range(table_ref.shape[1]):
        found = found + jnp.where(table_ref[:, m : m + 1] == page, code_ref[:, m : m + 1], 0.0)
    code = jnp.sum(found, axis=0, keepdims=True)
    owner = jnp.floor(code * (1.0 / 32.0))
    live = code - 32.0 * owner
    which = lax.broadcasted_iota(jnp.int32, (16, step_pages), 0)
    both = jnp.where(which == 0, owner, live).astype(jnp.bfloat16)
    spread = jnp.dot(both, spread_ref[...], preferred_element_type=jnp.float32)
    position = lax.broadcasted_iota(jnp.int32, (1, tokens), 1) % page_size
    token_owner = jnp.where(position.astype(jnp.float32) < spread[1:2], spread[0:1], -1.0)

    row_id = lax.broadcasted_iota(jnp.int32, (group * rows, 1), 0)
    row_id = (row_id % rows).astype(jnp.float32)
    for c in range(copies):
        keys = pool_ref[:, c, 0].reshape(tokens, width)
        values = pool_ref[:, c, 1].reshape(tokens, width)
        scores = lax.dot_general(
            query_ref[c], keys, (((1,), (1,)), ((), ())), preferred_element_type=jnp.float32
        )
        scores = jnp.where(token_owner == row_id, scores, NEVER)
        before = top_ref[c, :, 0:1]
        highest = jnp.maximum(before, jnp.max(scores, axis=1, keepdims=True))
        decay = jnp.exp2((before - highest) * factor)
        weights = jnp.exp2((scores - highest) * factor)
        mass = jnp.sum(weights, axis=1, keepdims=True)
        context = jnp.dot(weights.astype(jnp.bfloat16), values, preferred_element_type=jnp.float32)
        top_ref[c] = jnp.broadcast_to(highest, top_ref.shape[1:])
        mass_ref[c] = mass_ref[c] * decay + mass
        sum_ref[c] = sum_ref[c] * decay + context

    @pl.when(step == pl.num_programs(0) - 1)
    def _():
        out_ref[...] = (sum_ref[...] / mass_ref[...]).astype(out_ref.dtype)


def attend(query, fresh, table, code, pool, rows):
    copies, total, width = query.shape
    pages, _, _, page_size, _ = pool.shape
    step_pages = next(n for n in (112, 128, 64, 32, 16, 8, 1) if pages % n == 0)
    tokens = step_pages * page_size
    spread = jnp.asarray(np.arange(tokens)[None, :] // page_size == np.arange(step_pages)[:, None], jnp.bfloat16)
    factor = width ** (-0.5) * math.log2(math.e)

    def fixed(array):
        return pl.BlockSpec(array.shape, lambda i, n=array.ndim: (0,) * n)

    return pl.pallas_call(
        functools.partial(attend_kernel, rows, total // rows, page_size, step_pages, factor),
        grid=(pages // step_pages,),
        in_specs=[fixed(a) for a in (query, fresh, table, code, spread)]
        + [pl.BlockSpec((step_pages,) + pool.shape[1:], lambda i: (i, 0, 0, 0, 0))],
        out_specs=fixed(query),
        out_shape=jax.ShapeDtypeStruct(query.shape, query.dtype),
        scratch_shapes=[pltpu.VMEM(query.shape, jnp.float32) for _ in range(3)],
        compiler_params=pltpu.CompilerParams(vmem_limit_bytes=48 * 2**20),
    )(query, fresh, table, code, spread, pool)


def on_device(
    queries, fresh_kv, kv_pool, page_table, lengths, mig_src, mig_dst, mig_count, residual, out_weight, norm_gain,
):
    tp_ranks = lax.axis_size("tp")
    slots, heads, width = queries.shape
    pages, copies, _, page_size, _ = kv_pool.shape
    group = heads // copies
    per_row = page_table.shape[1]
    ranks, capacity = mig_src.shape[1:]
    moves = capacity // per_row
    extra = ranks * moves
    rows = slots + extra

    listed = mig_dst[0].reshape(extra, per_row)
    used = (jnp.arange(moves)[None, :] * per_row < mig_count[0][:, None]).reshape(extra)
    same = listed[:, :, None, None] == page_table[None, None]
    place = jnp.sum(same * jnp.arange(per_row, dtype=jnp.int32), axis=(2, 3))
    chosen = jnp.any(same[:, 0], axis=2) & used[:, None]
    length = jnp.sum(chosen * lengths[None, :], axis=1)
    filled = jnp.clip(length[:, None] - place * page_size, 0, page_size)
    away = jnp.any(chosen, axis=0)
    pick = chosen.astype(jnp.bfloat16)
    query_rows = queries.reshape(slots, heads * width)
    fresh_rows = fresh_kv.reshape(slots, copies * 2 * width)
    payload = jnp.dot(pick, jnp.concatenate([query_rows, fresh_rows], axis=1), preferred_element_type=jnp.float32)
    payload = jnp.concatenate(
        [payload.astype(jnp.bfloat16), jnp.pad(filled, ((0, 0), (0, width - per_row))).astype(jnp.bfloat16)], axis=1
    )
    guest = lax.all_to_all(payload.reshape(ranks, moves, -1), "rep", split_axis=0, concat_axis=0, tiled=True)
    guest = guest.reshape(extra, -1)
    cut = heads * width
    query_all = jnp.concatenate([query_rows, guest[:, :cut]], axis=0)
    fresh_all = jnp.concatenate([fresh_rows, guest[:, cut : cut + copies * 2 * width]], axis=0)
    guest_filled = guest[:, cut + copies * 2 * width :][:, :per_row].astype(jnp.int32)
    table = jnp.concatenate([page_table, mig_src[0].reshape(extra, per_row)], axis=0)
    local = jnp.clip(
        lengths[:, None] - jnp.arange(per_row, dtype=jnp.int32)[None, :] * page_size, 0, page_size
    )
    local = jnp.where(away[:, None], 0, local)
    filled_all = jnp.concatenate([local, guest_filled], axis=0)
    table = jnp.where(filled_all > 0, table, -1)
    code = (jnp.arange(rows, dtype=jnp.int32)[:, None] * 32 + filled_all).astype(jnp.float32)
    query_all = query_all.reshape(rows, copies, group, width).transpose(1, 2, 0, 3).reshape(copies, group * rows, width)
    fresh_all = fresh_all.reshape(rows, copies, 2, width).transpose(1, 2, 0, 3)
    attended = attend(query_all, fresh_all, table, code, kv_pool, rows)
    attended = attended.reshape(copies, group, rows, width).transpose(2, 0, 1, 3).reshape(rows, heads * width)
    back = lax.all_to_all(attended[slots:].reshape(ranks, moves, -1), "rep", split_axis=0, concat_axis=0, tiled=True)
    home = lax.dot_general(
        pick, back.reshape(extra, -1), (((0,), (0,)), ((), ())), preferred_element_type=jnp.float32
    ).astype(jnp.bfloat16)
    attended = jnp.where(away[:, None], home, attended[:slots])

    model_width = out_weight.shape[1]
    local_width = model_width // tp_ranks
    feature_share = lax.psum_scatter(
        lax.dot_general(
            out_weight, attended, (((0,), (1,)), ((), ())), preferred_element_type=jnp.float32
        ),
        "tp",
        scatter_dimension=0,
        tiled=True,
    )
    mixed_out = feature_share.T + residual.astype(jnp.float32)
    squares = lax.psum(jnp.sum(mixed_out * mixed_out, axis=1), "tp")
    scaled = mixed_out * lax.rsqrt(squares / model_width + EPSILON)[:, None]
    local_gain = lax.dynamic_slice_in_dim(
        norm_gain, lax.axis_index("tp") * local_width, local_width, 0
    )
    return (local_gain.astype(jnp.float32)[None, :] * scaled).astype(jnp.bfloat16)


def solution(mesh):
    in_specs = (
        P(("parts", "rep"), "tp", None),
        P(("parts", "rep"), "tp", None, None),
        P(("parts", "rep"), "tp", None, None, None),
        P(("parts", "rep"), None),
        P(("parts", "rep")),
        P(("parts", "rep"), None, None),
        P(("parts", "rep"), None, None),
        P(("parts", "rep"), None),
        P(("parts", "rep"), "tp"),
        P("tp", None),
        P(),
    )
    out_specs = P(("parts", "rep"), "tp")
    return jax.shard_map(
        on_device, mesh=mesh, in_specs=in_specs, out_specs=out_specs, check_vma=False
    )
```

time: 278 us -> 194 us (0.70)
  local copies, waits for them, and re-layouts: 75.9 us -> 7.9 us
  waiting for transfers between devices: 137 us -> 114 us
  matrix products: 29.6 us -> 6.74 us
  Pallas kernels: 0 us -> 22.4 us
  other arithmetic: 5.93 us -> 10.3 us
  starting transfers between devices: 4.21 us -> 7.5 us
    gather x2 -> x0, local copies, waits for them, and re-layouts: 28.1 us -> none  [the longest x1 19.7 us: on_device(): page_blocks = moved_pool[page_table]]
    dot_general x2 -> x1, matrix products: 25.9 us -> 0.15 us  [on_device(): jnp.dot(pick, jnp.concatenate([query_rows, fresh_rows], axis=1), preferre...]
    pallas_call x0 -> x1, Pallas kernels: none -> 22.4 us  [attend(): pl.pallas_call(functools.partial(attend_kernel, rows, total // rows, page...]
    all_to_all x1 -> x2, waiting for transfers between devices: 24.7 us -> 3.54 us  [the longest x1 3.54 us: on_device(): lax.all_to_all(attended[slots:].reshape(ranks, moves, -1), 'rep', split_a...]
    scatter x1 -> x0, local copies, waits for them, and re-layouts: 16.9 us -> none  [on_device(): kv_pool.at[targets].set(incoming.reshape((-1,) + block_shape), mode='drop')]
    unnamed x21 -> x11, local copies, waits for them, and re-layouts: 17.3 us -> 3.51 us
    squeeze x2 -> x0, local copies, waits for them, and re-layouts: 11.4 us -> none  [the longest x1 11.3 us: on_device(): value_blocks = page_blocks[:, :, :, 1]]
    reduce_sum x1 -> x2, other arithmetic: 0.05 us -> 3.95 us  [the longest x1 3.18 us: on_device(): place = jnp.sum(same * jnp.arange(per_row, dtype=jnp.int32), axis=(2, 3))]
  transfers between devices with their start and end apart: 2 -> 3, of which waited for: 2 -> 2; matrix products, arithmetic and copies ran while one was open for 1% -> 3% of each run, Pallas kernels for 0% -> 0%
where the time goes in v1:
time: 194 us
  waiting for transfers between devices  114 us (59%)
  Pallas kernels  22.4 us (12%)
  between operations  13.6 us (7%)
  blocking collectives  10.9 us (6%)
  other arithmetic  10.3 us (5%)
  local copies, waits for them, and re-layouts  7.9 us (4%)
  starting transfers between devices  7.5 us (4%)
  matrix products  6.74 us (3%)
    reduce_scatter x1, waiting for transfers between devices, on_device(): lax.psum_scatter(lax.dot_general(out_weight, attended, (((0,), (1,)), (()...  111 us
    pallas_call x1, Pallas kernels, attend(): pl.pallas_call(functools.partial(attend_kernel, rows, total // rows, page...  22.4 us
    psum x1, blocking collectives, on_device(): squares = lax.psum(jnp.sum(mixed_out * mixed_out, axis=1), 'tp')  10.9 us
    dot_general x1, matrix products, on_device(): lax.dot_general(out_weight, attended, (((0,), (1,)), ((), ())), preferred...  6.6 us
    all_to_all x1, starting transfers between devices, on_device(): lax.all_to_all(payload.reshape(ranks, moves, -1), 'rep', split_axis=0, co...  4.21 us
  transfers between devices with their start and end apart: 3, of which 2 were waited for; matrix products, arithmetic and copies ran while one was open for 3% of the time, Pallas kernels for 0%

profile of v1, /device:TPU:0, one launch (start us, length us, event | category | flops | bytes accessed | tf_op | source)
XLA Modules:
  0.0 193.9 jit_solution(10065133345065638296)
XLA Ops:
  6.5 0.0 copy-start
  6.5 0.8 eq.15
  7.3 0.9 broadcast_compare_fusion
  8.2 3.2 %select_reduce_fusion = s32[16,8]{1,0:T(8,128)S(1)} fusion(s32[128,8]{0,1:T(8,128)} %param.15, s32[16,8]{1,0:T(8,128)S(1)} %eq.15), kind=kLoop, calls=%fused_computation.7 | loop fusion | flops 393088 | bytes 5120 | tf_op jit(solution)/shard_map/reduce_sum | solution.py:113
  11.5 0.7 broadcast_compare_fusion.1
  12.2 0.1 lt.30
  12.3 1.0 reshape.75
  13.2 0.9 copy.83
  14.1 0.1 fusion.9
  14.2 0.8 select_reduce_fusion.1
  15.0 0.1 clamp_convert_fusion
  15.0 0.1 convolution_convert_fusion.1
  15.2 0.6 reshape.76
  15.8 4.2 %all-to-all-start = ((bf16[4,4,896]{2,1,0:T(4,128)(2,1)}), bf16[4,4,896]{2,1,0:T(4,128)(2,1)S(1)}, u32[]{:S(2)}, u32[]{:S(2)}) async-start(bf16[4,4,896]{2,1,0:T(4,128)(2,1)} %reshape.76), calls=%async_computation | async-start | bytes 57344 | tf_op jit(solution)/shard_map/all_to_all | solution.py:125
  20.0 0.7 clamp_select_fusion
  20.8 0.8 copy.73
  21.6 0.9 copy.70
  22.5 0.9 copy.84
  23.3 0.8 reshape_squeeze.3
  24.1 0.0 all-to-all-done
  24.2 0.1 copy.79
  24.3 0.1 copy.74
  24.4 0.1 copy.75.code_ref
  24.6 0.0 copy-done
  24.6 22.4 %shard_map.118 = bf16[2,144,128]{2,1,0:T(8,128)(2,1)S(1)} custom-call(bf16[2,144,128]{2,1,0:T(8,128)(2,1)S(1)} %maximum_bitcast_fusion.1.query_ref, bf16[2,2,144,128]{3,2,1,0:T(8,128)(2,1)S(1)} %maximum_bitcast_fusion.fresh_ref, s32[144,8]{1,0:T(8,128)S(1)} %add_select_fusion.table_ref, f32[144,8]{1,0:T(8,128)S(1)} %copy.75.code_ref, ...), custom_call_target="tpu_custom_call" | custom-call | tf_op jit(solution)/shard_map/pallas_call | solution.py:85
  47.1 0.6 reshape.80
  47.7 3.3 %all-to-all-start.1 = ((bf16[4,4,256]{2,1,0:T(4,128)(2,1)}), bf16[4,4,256]{2,1,0:T(4,128)(2,1)S(1)}, u32[]{:S(2)}, u32[]{:S(2)}) async-start(bf16[4,4,256]{2,1,0:T(4,128)(2,1)} %reshape.80), calls=%async_computation.1 | async-start | bytes 16384 | tf_op jit(solution)/shard_map/all_to_all | solution.py:143
  51.0 0.0 reduce-scatter.2.cloned.1.call-start
  51.0 0.1 copy.77
  51.1 0.1 copy.78
  51.2 3.5 %all-to-all-done.1 = bf16[4,4,256]{2,1,0:T(4,128)(2,1)S(1)} async-done(((bf16[4,4,256]{2,1,0:T(4,128)(2,1)}), bf16[4,4,256]{2,1,0:T(4,128)(2,1)S(1)}, u32[]{:S(2)}, u32[]{:S(2)}) %all-to-all-start.1) | async-done | bytes 8224 | tf_op jit(solution)/shard_map/all_to_all | solution.py:143
  54.8 6.6 %convolution_bitcast_fusion = f32[12288,128]{0,1:T(8,128)} fusion(bf16[256,12288]{1,0:T(8,128)(2,1)} %param.21, bf16[128,256]{1,0:T(8,128)(2,1)S(1)} %copy.78, pred[16,128]{1,0:T(8,128)(4,1)S(1)} %get-tuple-element.6, bf16[16,256]{1,0:T(8,128)(2,1)S(1)} %reshape.81, pred[128]{0:T(512)(128)(4,1)S(1)} %get-tuple-element.5), kind=kOutput, calls=%fused_computation | convolution fusion | flops 806420480 | bytes 12658816 | tf_op jit(solution)/shard_map/dot_general | solution.py:152
  61.4 0.0 copy-start.2
  61.4 0.0 reduce-scatter.2.cloned.1.call-update
  61.4 0.8 dynamic-slice_convert_fusion
  62.2 110.9 %reduce-scatter.2.cloned.1.call-done = f32[3072,128]{0,1:T(8,128)} async-done(((f32[12288,128]{0,1:T(8,128)}), f32[3072,128]{0,1:T(8,128)}) %reduce-scatter.2.cloned.1.call-update) | async-done | bytes 1572880 | tf_op jit(solution)/shard_map/reduce_scatter | solution.py:151
  173.1 0.0 copy-done.2
  173.1 0.0 copy-start.1
  173.1 1.8 multiply_reduce_fusion
  175.0 10.9 %psum.7 = f32[128]{0:T(128)S(1)} all-reduce(f32[128]{0:T(128)S(1)} %multiply_reduce_fusion), channel_id=1, replica_groups=mesh['parts'=2,'rep'=4,'tp'=4] {'tp'}, use_global_device_ids=true, to_apply=%region_6.7 | all-reduce | flops 128 | bytes 1024 | tf_op jit(solution)/shard_map/psum | solution.py:160
  185.9 0.0 copy-done.1
  185.9 1.2 multiply_convert_fusion
  (24 shorter events, 0.2 us)
Async XLA Ops:
  6.5 18.1 %copy-start = (bf16[112,1792]{1,0:T(8,128)(2,1)S(1)}, bf16[112,1792]{1,0:T(8,128)(2,1)}, u32[]{:S(2)}) copy-start(bf16[112,1792]{1,0:T(8,128)(2,1)} %constant.36.clone.spread_ref) | copy-start | bytes 1204228
  15.8 8.3 %all-to-all-start = ((bf16[4,4,896]{2,1,0:T(4,128)(2,1)}), bf16[4,4,896]{2,1,0:T(4,128)(2,1)S(1)}, u32[]{:S(2)}, u32[]{:S(2)}) async-start(bf16[4,4,896]{2,1,0:T(4,128)(2,1)} %reshape.76), calls=%async_computation | async-start | bytes 57344 | tf_op jit(solution)/shard_map/all_to_all | solution.py:125
  47.7 7.1 %all-to-all-start.1 = ((bf16[4,4,256]{2,1,0:T(4,128)(2,1)}), bf16[4,4,256]{2,1,0:T(4,128)(2,1)S(1)}, u32[]{:S(2)}, u32[]{:S(2)}) async-start(bf16[4,4,256]{2,1,0:T(4,128)(2,1)} %reshape.80), calls=%async_computation.1 | async-start | bytes 16384 | tf_op jit(solution)/shard_map/all_to_all | solution.py:143
  51.0 122.2 %reduce-scatter.2.cloned.1.call-start = ((), (), s32[]{:S(2)}) async-start(), calls=%async_computation.3 | async-start | bytes 7864320 | tf_op jit(solution)/shard_map/reduce_scatter | solution.py:151
  61.4 111.7 %copy-start.2 = (bf16[128,3072]{1,0:T(8,128)(2,1)S(1)}, bf16[128,3072]{1,0:T(8,128)(2,1)}, u32[]{:S(2)}) copy-start(bf16[128,3072]{1,0:T(8,128)(2,1)} %param.20) | copy-start | bytes 2359300
  173.1 12.8 %copy-start.1 = (f32[3072,128]{0,1:T(8,128)S(1)}, f32[3072,128]{0,1:T(8,128)}, u32[]{:S(2)}) copy-start(f32[3072,128]{0,1:T(8,128)} %reduce-scatter.2.cloned.1.call-done) | copy-start | bytes 4718596
Sparse Core Ops, SparseCore 0:
  61.5 111.5 reduce-scatter.1

commit v2 on v0

v2 whole, which is shorter than its diff:
```python
import functools
import math

import jax
import jax.numpy as jnp
from jax import lax
from jax.experimental import pallas as pl
from jax.experimental.pallas import tpu as pltpu
from jax.sharding import PartitionSpec as P

EPSILON = 1e-05
NEVER = -1e30
MESH = pl.DeviceIdType.MESH
TILE = 8


def iota(shape, dimension):
    return lax.broadcasted_iota(jnp.int32, shape, dimension)


def exact_dot(left, right, contract):
    return lax.dot_general(
        left.astype(jnp.bfloat16), right.astype(jnp.bfloat16), (contract, ((), ())), preferred_element_type=jnp.float32
    )


def layer_kernel(
    ranks, tp, copies, group, step_pages, factor,
    inputs_ref, small_ref, table_ref, gain_ref, pool_hbm, residual_hbm, weight_hbm,
    out_ref,
    pool_ref, weight_ref, residual_ref, total_ref, spread_ref, query_ref, fresh_ref, place_ref, code_ref,
    top_ref, mass_ref, sum_ref, ask_ref, asked_ref, reply_ref, replied_ref, gathered_ref, square_ref, squares_ref,
    local_sem, pool_sem, ask_sem, reply_sem, gather_sem, square_sem, weight_send, weight_recv,
):
    slots, per_row = table_ref.shape
    pages, _, _, page_size, width = pool_hbm.shape
    steps = pages // step_pages
    tokens = step_pages * page_size
    heads = copies * group
    entries = small_ref.shape[1]
    capacity = entries // ranks
    moves = capacity // per_row
    extra = ranks * moves
    rows = slots + extra
    padded = ranks * TILE
    depth, local_width = weight_ref.shape[1:]
    segment = depth // (2 * ranks)
    half = segment // 2

    part = lax.axis_index("parts")
    me = lax.axis_index("rep")
    rank = lax.axis_index("tp")
    across_part = 1 - part
    across_rep = lax.rem(me + 2, ranks)
    mate = me + 1 - 2 * lax.rem(me, 2)

    def pool_copy(i):
        spot = pl.ds(i * step_pages, step_pages)
        return pltpu.make_async_copy(pool_hbm.at[spot], pool_ref.at[spot], pool_sem.at[i])

    def peer_rep(k):
        return lax.rem(me + k, ranks)

    def peer_tp(k):
        return lax.rem(rank + k, tp)

    def from_tp(k):
        return lax.rem(rank + tp - k, tp)

    def remote(src, dst, send, recv, **where):
        return pltpu.make_async_remote_copy(
            src_ref=src, dst_ref=dst, send_sem=send, recv_sem=recv, device_id=where, device_id_type=MESH
        )

    barrier = pltpu.get_barrier_semaphore()
    for k in range(1, ranks):
        pl.semaphore_signal(barrier, inc=1, device_id={"rep": peer_rep(k)}, device_id_type=MESH)

    def greet(k, _):
        pl.semaphore_signal(barrier, inc=1, device_id={"tp": peer_tp(k)}, device_id_type=MESH)
        return 0

    lax.fori_loop(1, tp, greet, 0)
    pl.semaphore_signal(barrier, inc=1, device_id={"parts": across_part}, device_id_type=MESH)

    pool_copy(0).start()
    pool_copy(1).start()

    target = small_ref[0:1, :]
    source = small_ref[1:2, :]
    count = small_ref[2:3, :]
    length = small_ref[3:4, :]
    valid = lax.rem(iota((1, entries), 1), capacity) < count
    listed = jnp.zeros((slots, entries), jnp.float32)
    spot_sum = jnp.zeros((slots, entries), jnp.float32)
    for m in range(per_row):
        same = jnp.where((table_ref[:, m : m + 1] == target) & valid, 1.0, 0.0)
        listed = listed + same
        spot_sum = spot_sum + float(m) * same
    length_row = length[:, :slots].astype(jnp.float32)
    diagonal = iota((slots, slots), 0) == iota((slots, slots), 1)
    length_column = jnp.sum(jnp.where(diagonal, length_row, 0.0), axis=1, keepdims=True)
    spot = jnp.sum(spot_sum, axis=0, keepdims=True)
    entry_length = jnp.sum(listed * length_column, axis=0, keepdims=True)
    filled = jnp.clip(entry_length - page_size * spot, 0.0, float(page_size))
    away = jnp.max(listed, axis=1, keepdims=True)
    row = iota((padded, entries), 0)
    column = iota((padded, entries), 1)
    first = row // TILE * capacity + lax.rem(row, TILE) * per_row
    real = lax.rem(row, TILE) < moves
    head_entry = jnp.where((column == first) & real, 1.0, 0.0)
    pick = exact_dot(head_entry, listed, ((1,), (1,)))
    asking = exact_dot(pick, inputs_ref[...], ((1,), (0,)))
    within = jnp.where((column >= first) & (column < first + per_row) & real, filled, 0.0)
    fold = jnp.where(lax.rem(iota((entries, width), 0), per_row) == iota((entries, width), 1), 1.0, 0.0)
    asking_filled = exact_dot(within, fold, ((1,), (0,)))
    asked_width = inputs_ref.shape[1]
    for d in range(ranks):
        ask_ref[d, :, :asked_width] = asking[d * TILE : (d + 1) * TILE]
        ask_ref[d, :, asked_width:] = asking_filled[d * TILE : (d + 1) * TILE]

    pl.semaphore_wait(barrier, ranks + tp - 1)

    def ask(k):
        return remote(ask_ref.at[peer_rep(k)], asked_ref.at[me], ask_sem.at[0, k], ask_sem.at[1, k], rep=peer_rep(k))

    for k in range(1, ranks):
        ask(k).start()

    mine = part * ranks + me

    def piece(t, owner_part, owner_rep, start=0, size=segment):
        begin = pl.multiple_of((owner_part * ranks + owner_rep) * segment + start, half)
        return weight_ref.at[t, pl.ds(begin, size)]

    def hop(kind, k, spot_ref, **where):
        return remote(spot_ref, spot_ref, weight_send.at[kind, k], weight_recv.at[kind, k], **where)

    def spread_first(k):
        other = peer_tp(k)
        begin = pl.multiple_of(mine * segment, segment)
        columns = pl.ds(pl.multiple_of(other * local_width, 128), local_width)
        return remote(
            weight_hbm.at[pl.ds(begin, segment), columns], piece(rank, part, me),
            weight_send.at[0, k], weight_recv.at[0, k], tp=other,
        )

    def own_first(k):
        return hop(1, k, piece(from_tp(k), part, me), rep=across_rep)

    def own_second(k):
        return hop(2, k, piece(from_tp(k), part, me), parts=across_part)

    def own_mate(k):
        return hop(3, k, piece(from_tp(k), part, me), rep=mate)

    def pass_first(k):
        return hop(4, k, piece(from_tp(k), part, across_rep, 0, half), parts=across_part)

    def pass_second(k):
        return hop(5, k, piece(from_tp(k), across_part, me, half, half), rep=across_rep)

    def first_mate(k):
        return hop(6, k, piece(from_tp(k), part, across_rep), rep=mate)

    def second_mate(k):
        return hop(7, k, piece(from_tp(k), across_part, me), rep=mate)

    def corner_mate(k):
        return hop(8, k, piece(from_tp(k), across_part, across_rep), rep=mate)

    def arrival(kind, k, spot_ref):
        hop(kind, k, spot_ref, rep=mate).wait_recv()

    def loop(low, high, body):
        def run(k, _):
            body(k)
            return 0

        lax.fori_loop(low, high, run, 0)

    def stage_one(k):
        arrival(0, k, piece(from_tp(k), part, me))
        own_first(k).start()
        own_second(k).start()
        own_mate(k).start()

    def stage_two(k):
        arrival(1, k, piece(from_tp(k), part, across_rep))
        arrival(2, k, piece(from_tp(k), across_part, me))
        pass_first(k).start()
        pass_second(k).start()
        first_mate(k).start()
        second_mate(k).start()

    def stage_three(k):
        arrival(4, k, piece(from_tp(k), across_part, across_rep, 0, half))
        arrival(5, k, piece(from_tp(k), across_part, across_rep, half, half))
        corner_mate(k).start()

    def stage_end(k):
        mate_rep = lax.rem(mate + 2, ranks)
        arrival(3, k, piece(from_tp(k), part, mate))
        arrival(6, k, piece(from_tp(k), part, mate_rep))
        arrival(7, k, piece(from_tp(k), across_part, mate))
        arrival(8, k, piece(from_tp(k), across_part, mate_rep))
        for copy in (
            spread_first, own_first, own_second, own_mate, pass_first, pass_second, first_mate, second_mate, corner_mate,
        ):
            copy(k).wait_send()

    loop(1, tp, lambda k: spread_first(k).start())

    for i in range(2, steps):
        pool_copy(i).start()
    own_columns = pl.ds(pl.multiple_of(rank * local_width, 128), local_width)
    own_weight = pltpu.make_async_copy(weight_hbm.at[:, own_columns], weight_ref.at[rank], local_sem.at[0])
    own_weight.start()
    load_residual = pltpu.make_async_copy(residual_hbm, residual_ref, local_sem.at[1])
    load_residual.start()

    spread_ref[...] = jnp.where(
        iota((step_pages, tokens), 1) // page_size == iota((step_pages, tokens), 0), 1.0, 0.0
    ).astype(jnp.bfloat16)
    local_filled = jnp.clip(length_column - float(page_size) * iota((slots, per_row), 1).astype(jnp.float32), 0.0, float(page_size))
    local_filled = local_filled * (1.0 - away)
    place_ref[:slots, :] = table_ref[...]
    code_ref[:slots, :] = jnp.where(
        local_filled > 0.0, iota((slots, per_row), 0).astype(jnp.float32) * 32.0 + local_filled, 0.0
    )
    lanes = iota((extra, entries), 1)
    order = iota((extra, entries), 0)
    for m in range(per_row):
        found = jnp.where(lanes == order * per_row + m, source.astype(jnp.float32), 0.0)
        place_ref[slots:, m : m + 1] = jnp.sum(found, axis=1, keepdims=True).astype(jnp.int32)
    for h in range(heads):
        c, g = h // group, h % group
        query_ref[c, g * rows : g * rows + slots] = inputs_ref[:, h * width : (h + 1) * width]
    for c in range(copies):
        for i in range(2):
            begin = (heads + 2 * c + i) * width
            fresh_ref[c, i, :slots] = inputs_ref[:, begin : begin + width]

    asked_ref[pl.ds(me, 1)] = jnp.zeros((1,) + asked_ref.shape[1:], jnp.float32)
    for k in range(1, ranks):
        come = lax.rem(me + ranks - k, ranks)
        remote(asked_ref.at[come], asked_ref.at[come], ask_sem.at[0, k], ask_sem.at[1, k], rep=come).wait_recv()
    asked = asked_ref[...].reshape(padded, asked_ref.shape[2])
    row = iota((extra, padded), 0)
    pack = jnp.where(iota((extra, padded), 1) == row // moves * TILE + lax.rem(row, moves), 1.0, 0.0)
    guests = exact_dot(pack, asked, ((1,), (0,)))
    for h in range(heads):
        c, g = h // group, h % group
        query_ref[c, g * rows + slots : (g + 1) * rows] = guests[:, h * width : (h + 1) * width].astype(jnp.bfloat16)
    for c in range(copies):
        for i in range(2):
            begin = (heads + 2 * c + i) * width
            fresh_ref[c, i, slots:] = guests[:, begin : begin + width].astype(jnp.bfloat16)
    guest_filled = guests[:, asked_width : asked_width + per_row]
    code_ref[slots:, :] = jnp.where(
        guest_filled > 0.0, (iota((extra, per_row), 0) + slots).astype(jnp.float32) * 32.0 + guest_filled, 0.0
    )

    for c in range(copies):
        fresh_key = fresh_ref[c, 0].astype(jnp.float32)
        fresh_value = fresh_ref[c, 1].astype(jnp.float32)
        for g in range(group):
            span = slice(g * rows, (g + 1) * rows)
            own = jnp.sum(query_ref[c, span].astype(jnp.float32) * fresh_key, axis=1, keepdims=True)
            top_ref[c, span] = jnp.broadcast_to(own, (rows, width))
            mass_ref[c, span] = jnp.ones((rows, width), jnp.float32)
            sum_ref[c, span] = fresh_value

    def attend(step, _):
        pool_copy(step).wait()
        page = iota((rows, step_pages), 1) + step * step_pages
        found = jnp.zeros((rows, step_pages), jnp.float32)
        for m in range(per_row):
            found = found + jnp.where(place_ref[:, m : m + 1] == page, code_ref[:, m : m + 1], 0.0)
        code = jnp.sum(found, axis=0, keepdims=True)
        owner = jnp.floor(code * (1.0 / 32.0))
        live = code - 32.0 * owner
        both = jnp.where(iota((16, step_pages), 0) == 0, owner, live)
        spread = exact_dot(both, spread_ref[...], ((1,), (0,)))
        position = lax.rem(iota((1, tokens), 1), page_size).astype(jnp.float32)
        token_owner = jnp.where(position < spread[1:2], spread[0:1], -1.0)
        row_id = lax.rem(iota((group * rows, 1), 0), rows).astype(jnp.float32)
        chunk = pl.ds(step * step_pages, step_pages)
        for c in range(copies):
            keys = pool_ref[chunk, c, 0].reshape(tokens, width)
            values = pool_ref[chunk, c, 1].reshape(tokens, width)
            scores = lax.dot_general(
                query_ref[c], keys, (((1,), (1,)), ((), ())), preferred_element_type=jnp.float32
            )
            scores = jnp.where(token_owner == row_id, scores, NEVER)
            before = top_ref[c, :, 0:1]
            highest = jnp.maximum(before, jnp.max(scores, axis=1, keepdims=True))
            decay = jnp.exp2((before - highest) * factor)
            weights = jnp.exp2((scores - highest) * factor)
            mass = jnp.sum(weights, axis=1, keepdims=True)
            context = jnp.dot(weights.astype(jnp.bfloat16), values, preferred_element_type=jnp.float32)
            top_ref[c] = jnp.broadcast_to(highest, top_ref.shape[1:])
            mass_ref[c] = mass_ref[c] * decay + mass
            sum_ref[c] = sum_ref[c] * decay + context

        for j in range(3):
            low, high = (tp - 1) * j // 3 + 1, (tp - 1) * (j + 1) // 3 + 1
            pl.when(step == 2 + 2 * j)(lambda low=low, high=high: loop(low, high, stage_one))
            pl.when(step == 4 + 2 * j)(lambda low=low, high=high: loop(low, high, stage_two))
            if j < 2:
                pl.when(step == 6 + 2 * j)(lambda low=low, high=high: loop(low, high, stage_three))
        return 0

    lax.fori_loop(0, steps, attend, 0)

    unpack = jnp.where(
        (iota((padded, extra), 1) == iota((padded, extra), 0) // TILE * moves + lax.rem(iota((padded, extra), 0), TILE))
        & (lax.rem(iota((padded, extra), 0), TILE) < moves),
        1.0, 0.0,
    )
    attended = []
    for h in range(heads):
        c, g = h // group, h % group
        span = slice(g * rows, (g + 1) * rows)
        head = (sum_ref[c, span] / mass_ref[c, span]).astype(jnp.bfloat16)
        answer = exact_dot(unpack, head[slots:], ((1,), (0,)))
        for d in range(ranks):
            reply_ref[d, :, h * width : (h + 1) * width] = answer[d * TILE : (d + 1) * TILE]
        attended.append(head[:slots])

    def reply(k):
        return remote(
            reply_ref.at[peer_rep(k)], replied_ref.at[me], reply_sem.at[0, k], reply_sem.at[1, k], rep=peer_rep(k)
        )

    for k in range(1, ranks):
        reply(k).start()
    replied_ref[pl.ds(me, 1)] = jnp.zeros((1,) + replied_ref.shape[1:], jnp.float32)
    for k in range(1, ranks):
        come = lax.rem(me + ranks - k, ranks)
        remote(replied_ref.at[come], replied_ref.at[come], reply_sem.at[0, k], reply_sem.at[1, k], rep=come).wait_recv()
    home = exact_dot(pick, replied_ref[...].reshape(padded, heads * width), ((0,), (0,)))
    for h in range(heads):
        full = jnp.where(away > 0.0, home[:, h * width : (h + 1) * width], attended[h].astype(jnp.float32))
        gathered_ref[pl.ds(rank, 1), :, h * width : (h + 1) * width] = full.astype(jnp.bfloat16)[None]

    def gather(k):
        return remote(
            gathered_ref.at[rank], gathered_ref.at[rank], gather_sem.at[0, k], gather_sem.at[1, k], tp=peer_tp(k)
        )

    loop(1, tp, lambda k: gather(k).start())
    loop((tp - 1) * 2 // 3 + 1, tp, stage_three)
    loop(1, tp, stage_end)
    own_weight.wait()
    load_residual.wait()

    def gathered(k):
        spot_ref = gathered_ref.at[from_tp(k)]
        remote(spot_ref, spot_ref, gather_sem.at[0, k], gather_sem.at[1, k], tp=from_tp(k)).wait_recv()

    loop(1, tp, gathered)

    strip = next(n for n in (512, 384, 256, 128) if local_width % n == 0)
    square_sum = jnp.zeros((slots, 1), jnp.float32)
    for begin in range(0, local_width, strip):
        span = slice(begin, begin + strip)

        def add(t, total):
            return total + jnp.dot(gathered_ref[t], weight_ref[t, :, span], preferred_element_type=jnp.float32)

        total = residual_ref[:, span].astype(jnp.float32)
        if tp <= 4:
            for t in range(tp):
                total = add(t, total)
        else:
            total = lax.fori_loop(0, tp, add, total)
        total_ref[:, span] = total
        square_sum = square_sum + jnp.sum(total * total, axis=1, keepdims=True)
    square_row = jnp.sum(jnp.where(diagonal, square_sum, 0.0), axis=0, keepdims=True)
    square_ref[...] = jnp.broadcast_to(square_row, square_ref.shape)

    def share(k):
        return remote(square_ref, squares_ref.at[rank], square_sem.at[0, k], square_sem.at[1, k], tp=peer_tp(k))

    loop(1, tp, lambda k: share(k).start())
    squares_ref[pl.ds(rank, 1)] = jnp.broadcast_to(square_row, (1,) + square_ref.shape)

    def shared(k):
        spot_ref = squares_ref.at[from_tp(k)]
        remote(spot_ref, spot_ref, square_sem.at[0, k], square_sem.at[1, k], tp=from_tp(k)).wait_recv()

    loop(1, tp, shared)
    all_row = jnp.sum(squares_ref[...], axis=0)[0:1]
    all_column = jnp.sum(jnp.where(diagonal, all_row, 0.0), axis=1, keepdims=True)
    scale = lax.rsqrt(all_column / (local_width * tp) + EPSILON)
    for begin in range(0, local_width, strip):
        span = slice(begin, begin + strip)
        out_ref[:, span] = (gain_ref[:, span] * (total_ref[:, span] * scale)).astype(out_ref.dtype)

    for k in range(1, ranks):
        ask(k).wait_send()
        reply(k).wait_send()

    def finish(k):
        gather(k).wait_send()
        share(k).wait_send()

    loop(1, tp, finish)


def on_device(
    queries, fresh_kv, kv_pool, page_table, lengths, mig_src, mig_dst, mig_count, residual, out_weight, norm_gain,
):
    tp = lax.axis_size("tp")
    slots, heads, width = queries.shape
    pages, copies, _, page_size, _ = kv_pool.shape
    group = heads // copies
    per_row = page_table.shape[1]
    ranks, capacity = mig_src.shape[1:]
    extra = ranks * capacity // per_row
    rows = slots + extra
    depth, model_width = out_weight.shape
    local_width = model_width // tp
    step_pages = next(n for n in (112, 128, 64, 32, 16) if pages % n == 0)
    tokens = step_pages * page_size
    factor = width ** (-0.5) * math.log2(math.e)

    inputs = jnp.concatenate(
        [queries.reshape(slots, heads * width), fresh_kv.reshape(slots, copies * 2 * width)], axis=1
    )
    small = jnp.stack([
        mig_dst.reshape(-1), mig_src.reshape(-1), jnp.repeat(mig_count[0], capacity), lengths,
    ])
    gain = lax.dynamic_slice_in_dim(norm_gain, lax.axis_index("tp") * local_width, local_width, 0)
    gain = gain.astype(jnp.float32)[None, :]

    vmem = pl.BlockSpec(memory_space=pltpu.VMEM)
    anywhere = pl.BlockSpec(memory_space=pl.ANY)
    scratch = lambda shape, kind: pltpu.VMEM(shape, kind)
    payload = inputs.shape[1] + width
    return pl.pallas_call(
        functools.partial(layer_kernel, ranks, tp, copies, group, step_pages, factor),
        in_specs=[vmem] * 4 + [anywhere] * 3,
        out_specs=vmem,
        out_shape=jax.ShapeDtypeStruct((slots, local_width), jnp.bfloat16),
        scratch_shapes=[
            scratch(kv_pool.shape, jnp.bfloat16),
            scratch((tp, depth, local_width), jnp.bfloat16),
            scratch((slots, local_width), jnp.bfloat16),
            scratch((slots, local_width), jnp.float32),
            scratch((step_pages, tokens), jnp.bfloat16),
            scratch((copies, group * rows, width), jnp.bfloat16),
            scratch((copies, 2, rows, width), jnp.bfloat16),
            scratch((rows, per_row), jnp.int32),
            scratch((rows, per_row), jnp.float32),
            scratch((copies, group * rows, width), jnp.float32),
            scratch((copies, group * rows, width), jnp.float32),
            scratch((copies, group * rows, width), jnp.float32),
            scratch((ranks, TILE, payload), jnp.float32),
            scratch((ranks, TILE, payload), jnp.float32),
            scratch((ranks, TILE, heads * width), jnp.float32),
            scratch((ranks, TILE, heads * width), jnp.float32),
            scratch((tp, slots, heads * width), jnp.bfloat16),
            scratch((TILE, slots), jnp.float32),
            scratch((tp, TILE, slots), jnp.float32),
            pltpu.SemaphoreType.DMA((2,)),
            pltpu.SemaphoreType.DMA((pages // step_pages,)),
            pltpu.SemaphoreType.DMA((2, ranks)),
            pltpu.SemaphoreType.DMA((2, ranks)),
            pltpu.SemaphoreType.DMA((2, tp)),
            pltpu.SemaphoreType.DMA((2, tp)),
            pltpu.SemaphoreType.DMA((9, tp)),
            pltpu.SemaphoreType.DMA((9, tp)),
        ],
        compiler_params=pltpu.CompilerParams(
            collective_id=0, has_side_effects=True, vmem_limit_bytes=56 * 2**20
        ),
    )(inputs, small, page_table, gain, kv_pool, residual, out_weight)


def solution(mesh):
    in_specs = (
        P(("parts", "rep"), "tp", None),
        P(("parts", "rep"), "tp", None, None),
        P(("parts", "rep"), "tp", None, None, None),
        P(("parts", "rep"), None),
        P(("parts", "rep")),
        P(("parts", "rep"), None, None),
        P(("parts", "rep"), None, None),
        P(("parts", "rep"), None),
        P(("parts", "rep"), "tp"),
        P("tp", None),
        P(),
    )
    out_specs = P(("parts", "rep"), "tp")
    return jax.shard_map(
        on_device, mesh=mesh, in_specs=in_specs, out_specs=out_specs, check_vma=False
    )
```

time: 278 us -> 69.5 us (0.25)
  waiting for transfers between devices: 137 us -> 0 us
  local copies, waits for them, and re-layouts: 75.9 us -> 7.61 us
  Pallas kernels: 0 us -> 58.3 us
  matrix products: 29.6 us -> 0 us
  between operations: 13.6 us -> 0.02 us
  blocking collectives: 10.9 us -> 0 us
  starting transfers between devices: 4.21 us -> 0 us
    reduce_scatter x1 -> x0, waiting for transfers between devices: 112 us -> none  [on_device(): lax.psum_scatter(lax.dot_general(out_weight, attended, (((0,), (1,)), (()...]
    pallas_call x0 -> x1, Pallas kernels: none -> 58.3 us  [on_device(): pl.pallas_call(functools.partial(layer_kernel, ranks, tp, copies, group,...]
    dot_general x3 -> x0, matrix products: 29.6 us -> none  [the longest x1 19.5 us: on_device(): jnp.einsum('scgd,smcpd->scgmp', query_groups, key_blocks, preferred_eleme...]
    gather x2 -> x0, local copies, waits for them, and re-layouts: 28.1 us -> none  [the longest x1 19.7 us: on_device(): page_blocks = moved_pool[page_table]]
    all_to_all x1 -> x0, waiting for transfers between devices: 24.7 us -> none  [on_device(): lax.all_to_all(outgoing, 'rep', split_axis=0, concat_axis=0, tiled=True)]
    scatter x1 -> x0, local copies, waits for them, and re-layouts: 16.9 us -> none  [on_device(): kv_pool.at[targets].set(incoming.reshape((-1,) + block_shape), mode='drop')]
    unnamed x21 -> x3, local copies, waits for them, and re-layouts: 17.3 us -> 4.32 us
    squeeze x2 -> x0, local copies, waits for them, and re-layouts: 11.4 us -> none  [the longest x1 11.3 us: on_device(): value_blocks = page_blocks[:, :, :, 1]]
  transfers between devices with their start and end apart: 2 -> 0, of which waited for: 2 -> 0; matrix products, arithmetic and copies ran while one was open for 1% -> 0% of each run, Pallas kernels for 0% -> 0%
where the time goes in v2:
time: 69.5 us; the launch traced here: 69.2 us
  Pallas kernels  58.3 us (84%)
  local copies, waits for them, and re-layouts  7.61 us (11%)
  other arithmetic  3.22 us (5%)
    pallas_call x1, Pallas kernels, on_device(): pl.pallas_call(functools.partial(layer_kernel, ranks, tp, copies, group,...  58.3 us
    unnamed x3, local copies, waits for them, and re-layouts  4.32 us
    another operation x3, local copies, waits for them, and re-layouts, on_device(): jnp.stack([mig_dst.reshape(-1), mig_src.reshape(-1), jnp.repeat(mig_count...  1.61 us

profile of v2, /device:TPU:0, one launch (start us, length us, event | category | flops | bytes accessed | tf_op | source)
XLA Modules:
  0.0 69.2 jit_solution(14221933208713128552)
XLA Ops:
  0.0 0.8 %stack_reshape.10 = s32[1,128]{1,0:T(1,128)S(1)} reshape(s32[1,4,32]{2,1,0:T(4,128)} %param.16) | data formatting | bytes 1024 | tf_op jit(solution)/shard_map/stack;reshape | solution.py:432
  0.8 0.8 %stack_reshape.9 = s32[1,128]{1,0:T(1,128)S(1)} reshape(s32[1,4,32]{2,1,0:T(4,128)} %param.17) | data formatting | bytes 1024 | tf_op jit(solution)/shard_map/stack;reshape | solution.py:432
  1.5 0.7 %broadcast_in_dim.8 = s32[4,32]{1,0:T(4,128)S(1)} broadcast(s32[4]{0:T(128)} %bitcast.10), dimensions={0} | broadcast | bytes 528 | tf_op jit(solution)/shard_map/broadcast_in_dim | solution.py:433
  2.3 0.1 stack_reshape.11
  2.3 1.2 %pad_add_fusion.small_ref = s32[4,128]{1,0:T(4,128)} fusion(s32[1,128]{1,0:T(1,128)} %bitcast.11, s32[1,128]{1,0:T(1,128)S(1)} %stack_reshape.11, s32[1,128]{1,0:T(1,128)S(1)} %stack_reshape.10, s32[1,128]{1,0:T(1,128)S(1)} %stack_reshape.9), kind=kLoop, calls=%fused_computation.3 | loop fusion | flops 1536 | bytes 4096 | tf_op jit(solution)/shard_map/stack | solution.py:432
  3.6 1.3 %dynamic-slice_convert_fusion = f32[3072]{0:T(1024)} fusion(bf16[12288]{0:T(1024)(128)(2,1)} %param.21, s32[]{:T(128)S(6)} %select_n.3), kind=kLoop, calls=%fused_computation.2 | loop fusion | flops 3072 | bytes 18436 | tf_op jit(solution)/shard_map/broadcast_in_dim | solution.py:436
  4.9 0.8 %copy.15 = bf16[16,8,2,128]{3,1,2,0:T(8,128)(2,1)S(1)} copy(bf16[16,8,2,128]{3,2,1,0:T(2,128)(2,1)} %bitcast.8) | data formatting | bytes 131072
  5.7 1.4 %copy.12.table_ref = s32[128,8]{1,0:T(8,128)} copy(s32[128,8]{0,1:T(8,128)} %param.14) | data formatting | bytes 8192 | tf_op args[3]
  7.1 1.0 %reshape.7 = bf16[128,512]{1,0:T(8,128)(2,1)S(1)} reshape(bf16[128,2,2,128]{3,2,1,0:T(2,128)(2,1)} %param.12) | data formatting | bytes 262144 | tf_op jit(solution)/shard_map/reshape | solution.py:430
  8.1 0.7 pad_maximum_fusion.inputs_ref
  8.8 58.3 %shard_map.109 = bf16[128,3072]{1,0:T(8,128)(2,1)} custom-call(bf16[128,768]{1,0:T(8,128)(2,1)} %pad_maximum_fusion.inputs_ref, s32[4,128]{1,0:T(4,128)} %pad_add_fusion.small_ref, s32[128,8]{1,0:T(8,128)} %copy.12.table_ref, f32[1,3072]{1,0:T(1,128)} %bitcast.9, bf16[1120,2,2,16,128]{4,3,2,1,0:T(8,128)(2,1)} %pool_hbm.1, bf16[128,3072]{1,0:T(8,128)(2,1)} %residual_hbm.1, ...), custom_call_target="tpu_custom_call" | custom-call | tf_op jit(solution)/shard_map/pallas_call | solution.py:442
  67.1 2.1 %copy.17 = bf16[128,3072]{1,0:T(8,128)(2,1)} copy(bf16[128,3072]{1,0:T(8,128)(2,1)} %shard_map.109) | data formatting | bytes 1572864

commit v3 on v2

v3 whole, which is shorter than its diff:
```python
import functools
import math

import jax
import jax.numpy as jnp
from jax import lax
from jax.experimental import pallas as pl
from jax.experimental.pallas import tpu as pltpu
from jax.sharding import PartitionSpec as P

EPSILON = 1e-05
NEVER = -1e30
MESH = pl.DeviceIdType.MESH
TILE = 8


def iota(shape, dimension):
    return lax.broadcasted_iota(jnp.int32, shape, dimension)


def exact_dot(left, right, contract):
    return lax.dot_general(
        left.astype(jnp.bfloat16), right.astype(jnp.bfloat16), (contract, ((), ())), preferred_element_type=jnp.float32
    )


def layer_kernel(
    ranks, tp, copies, group, step_pages, factor,
    flat_query_ref, flat_fresh_ref, flat_table_ref, length_ref, source_ref, target_ref, count_ref, gain_ref,
    pool_hbm, residual_hbm, weight_hbm,
    out_ref, scale_ref,
    pool_ref, weight_ref, residual_ref, gains_ref, spread_ref, inputs_ref, query_ref, table_ref, code_ref,
    top_ref, mass_ref, sum_ref, guest_pages_ref, ask_ref, asked_ref, reply_ref, replied_ref, gathered_ref, square_ref,
    squares_ref,
    local_sem, pool_sem, ask_sem, reply_sem, gather_sem, square_sem, weight_send, weight_recv,
):
    slots, per_row = table_ref.shape
    pages, _, _, page_size, width = pool_hbm.shape
    steps = pages // step_pages
    tokens = step_pages * page_size
    heads = copies * group
    capacity = target_ref.shape[1]
    entries = ranks * capacity
    moves = capacity // per_row
    extra = ranks * moves
    rows = slots
    padded = ranks * TILE
    depth, local_width = weight_ref.shape[1:]
    segment = depth // (2 * ranks)
    half = segment // 2
    third = [((tp - 1) * j // 3 + 1, (tp - 1) * (j + 1) // 3 + 1) for j in range(3)]

    part = lax.axis_index("parts")
    me = lax.axis_index("rep")
    rank = lax.axis_index("tp")
    across_part = 1 - part
    across_rep = lax.rem(me + 2, ranks)
    mate = me + 1 - 2 * lax.rem(me, 2)

    def pool_copy(i):
        spot = pl.ds(i * step_pages, step_pages)
        return pltpu.make_async_copy(pool_hbm.at[spot], pool_ref.at[spot], pool_sem.at[i])

    def peer_rep(k):
        return lax.rem(me + k, ranks)

    def peer_tp(k):
        return lax.rem(rank + k, tp)

    def from_tp(k):
        return lax.rem(rank + tp - k, tp)

    def remote(src, dst, send, recv, **where):
        return pltpu.make_async_remote_copy(
            src_ref=src, dst_ref=dst, send_sem=send, recv_sem=recv, device_id=where, device_id_type=MESH
        )

    barrier = pltpu.get_barrier_semaphore()
    for k in range(1, ranks):
        pl.semaphore_signal(barrier, inc=1, device_id={"rep": peer_rep(k)}, device_id_type=MESH)

    def greet(k, _):
        pl.semaphore_signal(barrier, inc=1, device_id={"tp": peer_tp(k)}, device_id_type=MESH)
        return 0

    lax.fori_loop(1, tp, greet, 0)
    pl.semaphore_signal(barrier, inc=1, device_id={"parts": across_part}, device_id_type=MESH)

    pool_copy(0).start()
    pool_copy(1).start()

    def exact_columns(number, chosen, contract):
        high = jnp.floor(number * (1.0 / 64.0))
        low = number - 64.0 * high
        return 64.0 * exact_dot(high, chosen, contract) + exact_dot(low, chosen, contract)

    diagonal = iota((slots, slots), 0) == iota((slots, slots), 1)
    unit = jnp.where(diagonal, 1.0, 0.0)
    numbers = flat_table_ref[...].astype(jnp.float32)
    high = jnp.floor(numbers * (1.0 / 64.0))
    low = numbers - 64.0 * high
    columns_first = ((1,), (1,))
    table = 64.0 * exact_dot(unit, high, columns_first) + exact_dot(unit, low, columns_first)
    table_ref[...] = table.astype(jnp.int32)
    tile_up = jnp.where(
        iota((capacity, entries), 0) == lax.rem(iota((capacity, entries), 1), capacity), 1.0, 0.0
    )
    tiled = exact_columns(target_ref[...].astype(jnp.float32), tile_up, ((1,), (0,)))
    in_rank = iota((ranks, entries), 1) // capacity == iota((ranks, entries), 0)
    target = jnp.sum(jnp.where(in_rank, tiled, 0.0), axis=0, keepdims=True).astype(jnp.int32)
    count = jnp.zeros((1, entries), jnp.int32)
    for d in range(ranks):
        count = jnp.where(iota((1, entries), 1) // capacity == d, count_ref[:, d : d + 1], count)
    valid = lax.rem(iota((1, entries), 1), capacity) < count
    flat_query = flat_query_ref[...]
    flat_fresh = flat_fresh_ref[...]

    def take(flat, parts, i):
        size = flat.shape[0]
        chosen = jnp.where(iota((slots, size), 1) == iota((slots, size), 0) * parts + i, 1.0, 0.0)
        return exact_dot(chosen, flat, ((1,), (0,))).astype(jnp.bfloat16)

    for h in range(heads):
        rows_of_head = take(flat_query, heads, h)
        inputs_ref[:, h * width : (h + 1) * width] = rows_of_head
        query_ref[h // group, h % group * rows : (h % group + 1) * rows] = rows_of_head
    for i in range(2 * copies):
        inputs_ref[:, (heads + i) * width : (heads + i + 1) * width] = take(flat_fresh, 2 * copies, i)
    listed = jnp.zeros((slots, entries), jnp.float32)
    spot_sum = jnp.zeros((slots, entries), jnp.float32)
    for m in range(per_row):
        same = jnp.where((table_ref[:, m : m + 1] == target) & valid, 1.0, 0.0)
        listed = listed + same
        spot_sum = spot_sum + float(m) * same
    length_row = length_ref[...].astype(jnp.float32)
    length_column = jnp.sum(jnp.where(diagonal, length_row, 0.0), axis=1, keepdims=True)
    spot = jnp.sum(spot_sum, axis=0, keepdims=True)
    entry_length = jnp.sum(listed * length_column, axis=0, keepdims=True)
    filled = jnp.clip(entry_length - page_size * spot, 0.0, float(page_size))
    away = jnp.max(listed, axis=1, keepdims=True)
    row = iota((padded, entries), 0)
    column = iota((padded, entries), 1)
    first = row // TILE * capacity + lax.rem(row, TILE) * per_row
    real = lax.rem(row, TILE) < moves
    head_entry = jnp.where((column == first) & real, 1.0, 0.0)
    pick = exact_dot(head_entry, listed, ((1,), (1,)))
    asking = exact_dot(pick, inputs_ref[...], ((1,), (0,)))
    within = jnp.where((column >= first) & (column < first + per_row) & real, filled, 0.0)
    fold = jnp.where(lax.rem(iota((entries, width), 0), per_row) == iota((entries, width), 1), 1.0, 0.0)
    asking_filled = exact_dot(within, fold, ((1,), (0,)))
    asked_width = inputs_ref.shape[1]
    for d in range(ranks):
        ask_ref[d, :, :asked_width] = asking[d * TILE : (d + 1) * TILE]
        ask_ref[d, :, asked_width:] = asking_filled[d * TILE : (d + 1) * TILE]

    pl.semaphore_wait(barrier, ranks + tp - 1)

    def ask(k):
        return remote(ask_ref.at[peer_rep(k)], asked_ref.at[me], ask_sem.at[0, k], ask_sem.at[1, k], rep=peer_rep(k))

    for k in range(1, ranks):
        ask(k).start()

    mine = part * ranks + me

    def piece(t, owner_part, owner_rep, h):
        begin = pl.multiple_of((owner_part * ranks + owner_rep) * segment + h * half, half)
        return weight_ref.at[t, pl.ds(begin, half)]

    def hop(kind, k, h, spot_ref, **where):
        return remote(spot_ref, spot_ref, weight_send.at[kind, 2 * k + h], weight_recv.at[kind, 2 * k + h], **where)

    def spread_first(k, h):
        other = peer_tp(k)
        begin = pl.multiple_of(mine * segment + h * half, half)
        columns = pl.ds(pl.multiple_of(other * local_width, 128), local_width)
        return remote(
            weight_hbm.at[pl.ds(begin, half), columns], piece(rank, part, me, h),
            weight_send.at[0, 2 * k + h], weight_recv.at[0, 2 * k + h], tp=other,
        )

    def own_first(k, h):
        return hop(1, k, h, piece(from_tp(k), part, me, h), rep=across_rep)

    def own_second(k, h):
        return hop(2, k, h, piece(from_tp(k), part, me, h), parts=across_part)

    def own_mate(k, h):
        return hop(3, k, h, piece(from_tp(k), part, me, h), rep=mate)

    def corner(k, h):
        if h == 0:
            return hop(4, k, h, piece(from_tp(k), part, across_rep, h), parts=across_part)
        return hop(4, k, h, piece(from_tp(k), across_part, me, h), rep=across_rep)

    def first_mate(k, h):
        return hop(5, k, h, piece(from_tp(k), part, across_rep, h), rep=mate)

    def second_mate(k, h):
        return hop(6, k, h, piece(from_tp(k), across_part, me, h), rep=mate)

    def corner_mate(k, h):
        return hop(7, k, h, piece(from_tp(k), across_part, across_rep, h), rep=mate)

    def arrival(kind, k, h, spot_ref):
        hop(kind, k, h, spot_ref, rep=mate).wait_recv()

    def loop(low, high, body):
        def run(k, _):
            body(k)
            return 0

        lax.fori_loop(low, high, run, 0)

    def stage_one(k, h):
        arrival(0, k, h, piece(from_tp(k), part, me, h))
        own_first(k, h).start()
        own_second(k, h).start()
        own_mate(k, h).start()

    def stage_two(k, h):
        arrival(1, k, h, piece(from_tp(k), part, across_rep, h))
        arrival(2, k, h, piece(from_tp(k), across_part, me, h))
        corner(k, h).start()
        first_mate(k, h).start()
        second_mate(k, h).start()

    def stage_three(k, h):
        arrival(4, k, h, piece(from_tp(k), across_part, across_rep, h))
        corner_mate(k, h).start()

    def stage_end(k, h):
        mate_rep = lax.rem(mate + 2, ranks)
        arrival(3, k, h, piece(from_tp(k), part, mate, h))
        arrival(5, k, h, piece(from_tp(k), part, mate_rep, h))
        arrival(6, k, h, piece(from_tp(k), across_part, mate, h))
        arrival(7, k, h, piece(from_tp(k), across_part, mate_rep, h))
        for copy in (
            spread_first, own_first, own_second, own_mate, corner, first_mate, second_mate, corner_mate,
        ):
            copy(k, h).wait_send()

    def stage(body, j):
        loop(*third[j // 2], lambda k: body(k, j % 2))

    stage(lambda k, h: spread_first(k, h).start(), 0)
    stage(lambda k, h: spread_first(k, h).start(), 1)

    for i in range(2, steps):
        pool_copy(i).start()
    gains_ref[...] = gain_ref[...].astype(jnp.float32)
    own_columns = pl.ds(pl.multiple_of(rank * local_width, 128), local_width)
    own_weight = pltpu.make_async_copy(weight_hbm.at[:, own_columns], weight_ref.at[rank], local_sem.at[0])
    own_weight.start()
    load_residual = pltpu.make_async_copy(residual_hbm, residual_ref, local_sem.at[1])
    load_residual.start()

    spread_ref[...] = jnp.where(
        iota((step_pages, tokens), 1) // page_size == iota((step_pages, tokens), 0), 1.0, 0.0
    ).astype(jnp.bfloat16)
    local_filled = jnp.clip(length_column - float(page_size) * iota((slots, per_row), 1).astype(jnp.float32), 0.0, float(page_size))
    local_filled = local_filled * (1.0 - away)
    code_ref[...] = jnp.where(
        local_filled > 0.0, iota((slots, per_row), 0).astype(jnp.float32) * 32.0 + local_filled, 0.0
    )
    for c in range(copies):
        fresh_key = inputs_ref[:, (heads + 2 * c) * width : (heads + 2 * c + 1) * width].astype(jnp.float32)
        fresh_value = inputs_ref[:, (heads + 2 * c + 1) * width : (heads + 2 * c + 2) * width].astype(jnp.float32)
        for g in range(group):
            span = slice(g * rows, (g + 1) * rows)
            own = jnp.sum(query_ref[c, span].astype(jnp.float32) * fresh_key, axis=1, keepdims=True)
            top_ref[c, span] = jnp.broadcast_to(own, (rows, width))
            mass_ref[c, span] = jnp.ones((rows, width), jnp.float32)
            sum_ref[c, span] = fresh_value

    def serve():
        asked_ref[pl.ds(me, 1)] = jnp.zeros((1,) + asked_ref.shape[1:], jnp.float32)
        for k in range(1, ranks):
            come = lax.rem(me + ranks - k, ranks)
            remote(asked_ref.at[come], asked_ref.at[come], ask_sem.at[0, k], ask_sem.at[1, k], rep=come).wait_recv()

        def fetch(i, _):
            for j in range(per_row):
                e = i * per_row + j
                page = jnp.clip(source_ref[e // capacity, lax.rem(e, capacity)], 0, pages - 1)
                guest_pages_ref[pl.ds(e, 1)] = pool_ref[pl.ds(page, 1)]
            return 0

        lax.fori_loop(0, extra, fetch, 0)
        asked = asked_ref[...].reshape(padded, asked_ref.shape[2])
        row = iota((extra, padded), 0)
        pack = jnp.where(iota((extra, padded), 1) == row // moves * TILE + lax.rem(row, moves), 1.0, 0.0)
        guests = exact_dot(pack, asked, ((1,), (0,)))
        held = entries * page_size
        stretch = jnp.where(iota((width, held), 0) == lax.rem(iota((width, held), 1) // page_size, per_row), 1.0, 0.0)
        live = exact_dot(guests[:, asked_width : asked_width + width], stretch, ((1,), (0,)))
        token = iota((extra, held), 1)
        seen = (token // (per_row * page_size) == iota((extra, held), 0)) & (
            lax.rem(token, page_size).astype(jnp.float32) < live
        )
        unpack = jnp.where(
            (iota((padded, extra), 1) == iota((padded, extra), 0) // TILE * moves + lax.rem(iota((padded, extra), 0), TILE))
            & (lax.rem(iota((padded, extra), 0), TILE) < moves),
            1.0, 0.0,
        )
        for c in range(copies):
            fresh_key = guests[:, (heads + 2 * c) * width : (heads + 2 * c + 1) * width]
            fresh_value = guests[:, (heads + 2 * c + 1) * width : (heads + 2 * c + 2) * width]
            keys = guest_pages_ref[:, c, 0].reshape(held, width)
            values = guest_pages_ref[:, c, 1].reshape(held, width)
            for g in range(group):
                h = c * group + g
                query = guests[:, h * width : (h + 1) * width]
                own = jnp.sum(query * fresh_key, axis=1, keepdims=True)
                scores = lax.dot_general(
                    query.astype(jnp.bfloat16), keys, (((1,), (1,)), ((), ())), preferred_element_type=jnp.float32
                )
                scores = jnp.where(seen, scores, NEVER)
                highest = jnp.maximum(own, jnp.max(scores, axis=1, keepdims=True))
                weights = jnp.exp2((scores - highest) * factor)
                own_weight = jnp.exp2((own - highest) * factor)
                mass = own_weight + jnp.sum(weights, axis=1, keepdims=True)
                context = jnp.dot(weights.astype(jnp.bfloat16), values, preferred_element_type=jnp.float32)
                head = (context + own_weight * fresh_value) / mass
                answer = exact_dot(unpack, head, ((1,), (0,)))
                for d in range(ranks):
                    reply_ref[d, :, h * width : (h + 1) * width] = answer[d * TILE : (d + 1) * TILE]
        for k in range(1, ranks):
            reply(k).start()

    def reply(k):
        return remote(
            reply_ref.at[peer_rep(k)], replied_ref.at[me], reply_sem.at[0, k], reply_sem.at[1, k], rep=peer_rep(k)
        )

    middle = steps // 2

    def attend(step, _):
        pl.when(step < middle)(lambda: pool_copy(step).wait())
        page = iota((rows, step_pages), 1) + step * step_pages
        found = jnp.zeros((rows, step_pages), jnp.float32)
        for m in range(per_row):
            found = found + jnp.where(table_ref[:, m : m + 1] == page, code_ref[:, m : m + 1], 0.0)
        code = jnp.sum(found, axis=0, keepdims=True)
        owner = jnp.floor(code * (1.0 / 32.0))
        live = code - 32.0 * owner
        both = jnp.where(iota((16, step_pages), 0) == 0, owner, live)
        spread = exact_dot(both, spread_ref[...], ((1,), (0,)))
        position = lax.rem(iota((1, tokens), 1), page_size).astype(jnp.float32)
        token_owner = jnp.where(position < spread[1:2], spread[0:1], -1.0)
        row_id = lax.rem(iota((group * rows, 1), 0), rows).astype(jnp.float32)
        chunk = pl.ds(step * step_pages, step_pages)
        for c in range(copies):
            keys = pool_ref[chunk, c, 0].reshape(tokens, width)
            values = pool_ref[chunk, c, 1].reshape(tokens, width)
            scores = lax.dot_general(
                query_ref[c], keys, (((1,), (1,)), ((), ())), preferred_element_type=jnp.float32
            )
            scores = jnp.where(token_owner == row_id, scores, NEVER)
            before = top_ref[c, :, 0:1]
            highest = jnp.maximum(before, jnp.max(scores, axis=1, keepdims=True))
            decay = jnp.exp2((before - highest) * factor)
            weights = jnp.exp2((scores - highest) * factor)
            mass = jnp.sum(weights, axis=1, keepdims=True)
            context = jnp.dot(weights.astype(jnp.bfloat16), values, preferred_element_type=jnp.float32)
            top_ref[c] = jnp.broadcast_to(highest, top_ref.shape[1:])
            mass_ref[c] = mass_ref[c] * decay + mass
            sum_ref[c] = sum_ref[c] * decay + context

        for j in range(6):
            if j >= 2:
                pl.when(step == j - 1)(lambda j=j: stage(lambda k, h: spread_first(k, h).start(), j))
            pl.when(step == j + 2)(lambda j=j: stage(stage_one, j))
            if j + 4 < steps:
                pl.when(step == j + 4)(lambda j=j: stage(stage_two, j))
            if j + 6 < steps:
                pl.when(step == j + 6)(lambda j=j: stage(stage_three, j))
        return 0

    def pool_rest():
        for i in range(middle, steps):
            pool_copy(i).wait()
        serve()

    def both_parts(step, _):
        pl.when(step == middle)(pool_rest)
        return attend(step, 0)

    lax.fori_loop(0, steps, both_parts, 0)

    attended = []
    for h in range(heads):
        c, g = h // group, h % group
        span = slice(g * rows, (g + 1) * rows)
        head = (sum_ref[c, span] / mass_ref[c, span]).astype(jnp.bfloat16)
        attended.append(head)

    replied_ref[pl.ds(me, 1)] = jnp.zeros((1,) + replied_ref.shape[1:], jnp.float32)
    for k in range(1, ranks):
        come = lax.rem(me + ranks - k, ranks)
        remote(replied_ref.at[come], replied_ref.at[come], reply_sem.at[0, k], reply_sem.at[1, k], rep=come).wait_recv()
    home = exact_dot(pick, replied_ref[...].reshape(padded, heads * width), ((0,), (0,)))
    for h in range(heads):
        full = jnp.where(away > 0.0, home[:, h * width : (h + 1) * width], attended[h].astype(jnp.float32))
        gathered_ref[pl.ds(rank, 1), :, h * width : (h + 1) * width] = full.astype(jnp.bfloat16)[None]

    def gather(k):
        return remote(
            gathered_ref.at[rank], gathered_ref.at[rank], gather_sem.at[0, k], gather_sem.at[1, k], tp=peer_tp(k)
        )

    loop(1, tp, lambda k: gather(k).start())
    for j in range(6):
        if j + 4 >= steps:
            stage(stage_two, j)
    for j in range(6):
        if j + 6 >= steps:
            stage(stage_three, j)
    for j in range(6):
        stage(stage_end, j)
    own_weight.wait()
    load_residual.wait()

    def gathered(k):
        spot_ref = gathered_ref.at[from_tp(k)]
        remote(spot_ref, spot_ref, gather_sem.at[0, k], gather_sem.at[1, k], tp=from_tp(k)).wait_recv()

    loop(1, tp, gathered)

    strip = next(n for n in (512, 384, 256, 128) if local_width % n == 0)
    square_sum = jnp.zeros((slots, 1), jnp.float32)
    for begin in range(0, local_width, strip):
        span = slice(begin, begin + strip)

        def add(t, total):
            return total + jnp.dot(gathered_ref[t], weight_ref[t, :, span], preferred_element_type=jnp.float32)

        total = residual_ref[:, span].astype(jnp.float32)
        if tp <= 4:
            for t in range(tp):
                total = add(t, total)
        else:
            total = lax.fori_loop(0, tp, add, total)
        for j in range(0, strip, 128):
            tile = slice(begin + j, begin + j + 128)
            gain = gains_ref[pl.ds((rank * local_width + begin + j) // 128, 1), :]
            out_ref[:, tile] = total[:, j : j + 128] * gain
        square_sum = square_sum + jnp.sum(total * total, axis=1, keepdims=True)
    square_row = jnp.sum(jnp.where(diagonal, square_sum, 0.0), axis=0, keepdims=True)
    square_ref[...] = jnp.broadcast_to(square_row, square_ref.shape)

    def share(k):
        return remote(square_ref, squares_ref.at[rank], square_sem.at[0, k], square_sem.at[1, k], tp=peer_tp(k))

    loop(1, tp, lambda k: share(k).start())
    squares_ref[pl.ds(rank, 1)] = jnp.broadcast_to(square_row, (1,) + square_ref.shape)

    def shared(k):
        spot_ref = squares_ref.at[from_tp(k)]
        remote(spot_ref, spot_ref, square_sem.at[0, k], square_sem.at[1, k], tp=from_tp(k)).wait_recv()

    loop(1, tp, shared)
    all_row = jnp.sum(squares_ref[...], axis=0)[0:1]
    all_column = jnp.sum(jnp.where(diagonal, all_row, 0.0), axis=1, keepdims=True)
    scale_ref[...] = lax.rsqrt(all_column / (local_width * tp) + EPSILON)
    for k in range(1, ranks):
        ask(k).wait_send()
        reply(k).wait_send()

    def finish(k):
        gather(k).wait_send()
        share(k).wait_send()

    loop(1, tp, finish)


def on_device(
    queries, fresh_kv, kv_pool, page_table, lengths, mig_src, mig_dst, mig_count, residual, out_weight, norm_gain,
):
    tp = lax.axis_size("tp")
    slots, heads, width = queries.shape
    pages, copies, _, page_size, _ = kv_pool.shape
    group = heads // copies
    per_row = page_table.shape[1]
    ranks, capacity = mig_src.shape[1:]
    depth, model_width = out_weight.shape
    local_width = model_width // tp
    step_pages = next(n for n in (112, 128, 64, 32, 16) if pages % n == 0)
    tokens = step_pages * page_size
    factor = width ** (-0.5) * math.log2(math.e)

    vmem = pl.BlockSpec(memory_space=pltpu.VMEM)
    anywhere = pl.BlockSpec(memory_space=pl.ANY)
    scratch = lambda shape, kind: pltpu.VMEM(shape, kind)
    asked_width = (heads + 2 * copies) * width
    payload = asked_width + width
    total, scale = pl.pallas_call(
        functools.partial(layer_kernel, ranks, tp, copies, group, step_pages, factor),
        in_specs=[vmem] * 4 + [pl.BlockSpec(memory_space=pltpu.SMEM)] + [vmem] * 3 + [anywhere] * 3,
        out_specs=[vmem] * 2,
        out_shape=[
            jax.ShapeDtypeStruct((slots, local_width), jnp.float32), jax.ShapeDtypeStruct((slots, 1), jnp.float32),
        ],
        scratch_shapes=[
            scratch(kv_pool.shape, jnp.bfloat16),
            scratch((tp, depth, local_width), jnp.bfloat16),
            scratch((slots, local_width), jnp.bfloat16),
            scratch((model_width // 128, 128), jnp.float32),
            scratch((step_pages, tokens), jnp.bfloat16),
            scratch((slots, asked_width), jnp.bfloat16),
            scratch((copies, heads // copies * slots, width), jnp.bfloat16),
            scratch((slots, per_row), jnp.int32),
            scratch((slots, per_row), jnp.float32),
            scratch((copies, group * slots, width), jnp.float32),
            scratch((copies, group * slots, width), jnp.float32),
            scratch((copies, group * slots, width), jnp.float32),
            scratch((ranks * capacity,) + kv_pool.shape[1:], jnp.bfloat16),
            scratch((ranks, TILE, payload), jnp.float32),
            scratch((ranks, TILE, payload), jnp.float32),
            scratch((ranks, TILE, heads * width), jnp.float32),
            scratch((ranks, TILE, heads * width), jnp.float32),
            scratch((tp, slots, heads * width), jnp.bfloat16),
            scratch((TILE, slots), jnp.float32),
            scratch((tp, TILE, slots), jnp.float32),
            pltpu.SemaphoreType.DMA((2,)),
            pltpu.SemaphoreType.DMA((pages // step_pages,)),
            pltpu.SemaphoreType.DMA((2, ranks)),
            pltpu.SemaphoreType.DMA((2, ranks)),
            pltpu.SemaphoreType.DMA((2, tp)),
            pltpu.SemaphoreType.DMA((2, tp)),
            pltpu.SemaphoreType.DMA((8, 2 * tp)),
            pltpu.SemaphoreType.DMA((8, 2 * tp)),
        ],
        compiler_params=pltpu.CompilerParams(
            collective_id=0, has_side_effects=True, vmem_limit_bytes=56 * 2**20
        ),
    )(
        queries.reshape(-1, width), fresh_kv.reshape(-1, width), page_table.T, lengths[None, :], mig_src[0], mig_dst[0],
        mig_count, norm_gain.reshape(-1, 128), kv_pool, residual, out_weight,
    )
    return (total * scale).astype(jnp.bfloat16)


def solution(mesh):
    in_specs = (
        P(("parts", "rep"), "tp", None),
        P(("parts", "rep"), "tp", None, None),
        P(("parts", "rep"), "tp", None, None, None),
        P(("parts", "rep"), None),
        P(("parts", "rep")),
        P(("parts", "rep"), None, None),
        P(("parts", "rep"), None, None),
        P(("parts", "rep"), None),
        P(("parts", "rep"), "tp"),
        P("tp", None),
        P(),
    )
    out_specs = P(("parts", "rep"), "tp")
    return jax.shard_map(
        on_device, mesh=mesh, in_specs=in_specs, out_specs=out_specs, check_vma=False
    )
```

time: 69.5 us -> 54.1 us (0.78)
  Pallas kernels: 58.3 us -> 50.4 us
  local copies, waits for them, and re-layouts: 7.61 us -> 0 us
    pallas_call x1, Pallas kernels: 58.3 us -> 50.4 us  [on_device(): pl.pallas_call(functools.partial(layer_kernel, ranks, tp, copies, group,...]
    unnamed x3 -> x0, local copies, waits for them, and re-layouts: 4.32 us -> none
    convert_element_type x0 -> x1, other arithmetic: none -> 2.47 us  [on_device(): return (total * scale).astype(jnp.bfloat16)]
    another operation x3 -> x0, local copies, waits for them, and re-layouts: 1.61 us -> none  [on_device(): jnp.stack([mig_dst.reshape(-1), mig_src.reshape(-1), jnp.repeat(mig_count...]
    broadcast_in_dim x1 -> x0, other arithmetic: 1.29 us -> none  [on_device(): gain = gain.astype(jnp.float32)[None, :]]
    another operation x1 -> x0, other arithmetic: 1.24 us -> none  [on_device(): jnp.stack([mig_dst.reshape(-1), mig_src.reshape(-1), jnp.repeat(mig_count...]
    reshape x1 -> x0, local copies, waits for them, and re-layouts: 0.96 us -> none  [on_device(): fresh_kv.reshape(slots, copies * 2 * width)]
    pallas_call x0 -> x1, other arithmetic: none -> 0.94 us  [on_device(): pl.pallas_call(functools.partial(layer_kernel, ranks, tp, copies, group,...]
where the time goes in v3:
time: 54.1 us; the launch traced here: 53.9 us
  Pallas kernels  50.4 us (93%)
  other arithmetic  3.42 us (6%)
    pallas_call x1, Pallas kernels, on_device(): pl.pallas_call(functools.partial(layer_kernel, ranks, tp, copies, group,...  50.4 us
    convert_element_type x1, other arithmetic, on_device(): return (total * scale).astype(jnp.bfloat16)  2.47 us

profile of v3, /device:TPU:0, one launch (start us, length us, event | category | flops | bytes accessed | tf_op | source)
XLA Modules:
  0.0 53.9 jit_solution(7746319073950705985)
XLA Ops:
  0.0 50.4 %shard_map.109 = (f32[128,3072]{1,0:T(8,128)}, f32[128,1]{1,0:T(8,128)}) custom-call(bf16[256,128]{1,0:T(8,128)(2,1)} %bitcast.8, bf16[512,128]{1,0:T(8,128)(2,1)} %bitcast.7, s32[8,128]{1,0:T(8,128)} %bitcast.10, s32[1,128]{1,0:T(1,128)} %bitcast.13, s32[4,32]{1,0:T(4,128)} %bitcast.11, s32[4,32]{1,0:T(4,128)} %bitcast.12, s32[1,4]{1,0:T(1,128)} %count_ref.1, ...), custom_call_target="tpu_custom_call" | custom-call | tf_op jit(solution)/shard_map/pallas_call | solution.py:497
  50.4 0.9 %reduce = f32[128]{0:T(128)S(1)} reduce(f32[128,1]{1,0:T(8,128)} %get-tuple-element.8, f32[]{:T(128)} %constant.6), dimensions={1}, to_apply=%get-tuple-element.8.reduce_sub_computation | reduce | bytes 1028 | tf_op jit(solution)/shard_map/pallas_call | solution.py:497
  51.4 2.5 %multiply_convert_fusion = bf16[128,3072]{1,0:T(8,128)(2,1)} fusion(f32[128,3072]{1,0:T(8,128)} %get-tuple-element.7, f32[128]{0:T(128)S(1)} %reduce), kind=kLoop, calls=%fused_computation | loop fusion | flops 786432 | bytes 2359808 | tf_op jit(solution)/shard_map/convert_element_type | solution.py:541

commit v4 on v3

--- a/solution.py
+++ b/solution.py
@@ -28,8 +28,8 @@
     ranks, tp, copies, group, step_pages, factor,
     flat_query_ref, flat_fresh_ref, flat_table_ref, length_ref, source_ref, target_ref, count_ref, gain_ref,
     pool_hbm, residual_hbm, weight_hbm,
-    out_ref, scale_ref,
-    pool_ref, weight_ref, residual_ref, gains_ref, spread_ref, inputs_ref, query_ref, table_ref, code_ref,
+    result_ref,
+    out_ref, pool_ref, weight_ref, residual_ref, gains_ref, spread_ref, inputs_ref, query_ref, table_ref, code_ref,
     top_ref, mass_ref, sum_ref, guest_pages_ref, ask_ref, asked_ref, reply_ref, replied_ref, gathered_ref, square_ref,
     squares_ref,
     local_sem, pool_sem, ask_sem, reply_sem, gather_sem, square_sem, weight_send, weight_recv,
@@ -48,7 +48,7 @@
     depth, local_width = weight_ref.shape[1:]
     segment = depth // (2 * ranks)
     half = segment // 2
-    third = [((tp - 1) * j // 3 + 1, (tp - 1) * (j + 1) // 3 + 1) for j in range(3)]
+    third = [((tp - 1) * j // 3 + 1, (tp - 1) * (j + 1) // 3 + 1) for j in (0, 2, 1)]
 
     part = lax.axis_index("parts")
     me = lax.axis_index("rep")
@@ -88,6 +88,99 @@
 
     pool_copy(0).start()
     pool_copy(1).start()
+    pl.semaphore_wait(barrier, ranks + tp - 1)
+
+    mine = part * ranks + me
+
+    def piece(t, owner_part, owner_rep, h):
+        begin = pl.multiple_of((owner_part * ranks + owner_rep) * segment + h * half, half)
+        return weight_ref.at[t, pl.ds(begin, half)]
+
+    def hop(kind, k, h, spot_ref, **where):
+        return remote(spot_ref, spot_ref, weight_send.at[kind, 2 * k + h], weight_recv.at[kind, 2 * k + h], **where)
+
+    def spread_first(k, h):
+        other = peer_tp(k)
+        begin = pl.multiple_of(mine * segment + h * half, half)
+        columns = pl.ds(pl.multiple_of(other * local_width, 128), local_width)
+        return remote(
+            weight_hbm.at[pl.ds(begin, half), columns], piece(rank, part, me, h),
+            weight_send.at[0, 2 * k + h], weight_recv.at[0, 2 * k + h], tp=other,
+        )
+
+    def own_first(k, h):
+        return hop(1, k, h, piece(from_tp(k), part, me, h), rep=across_rep)
+
+    def own_second(k, h):
+        return hop(2, k, h, piece(from_tp(k), part, me, h), parts=across_part)
+
+    def own_mate(k, h):
+        return hop(3, k, h, piece(from_tp(k), part, me, h), rep=mate)
+
+    def corner(k, h):
+        if h == 0:
+            return hop(4, k, h, piece(from_tp(k), part, across_rep, h), parts=across_part)
+        return hop(4, k, h, piece(from_tp(k), across_part, me, h), rep=across_rep)
+
+    def first_mate(k, h):
+        return hop(5, k, h, piece(from_tp(k), part, across_rep, h), rep=mate)
+
+    def second_mate(k, h):
+        return hop(6, k, h, piece(from_tp(k), across_part, me, h), rep=mate)
+
+    def corner_mate(k, h):
+        return hop(7, k, h, piece(from_tp(k), across_part, across_rep, h), rep=mate)
+
+    def arrival(kind, k, h, spot_ref):
+        hop(kind, k, h, spot_ref, rep=mate).wait_recv()
+
+    def loop(low, high, body):
+        def run(k, _):
+            body(k)
+            return 0
+
+        lax.fori_loop(low, high, run, 0)
+
+    def stage_one(k, h):
+        arrival(0, k, h, piece(from_tp(k), part, me, h))
+        own_first(k, h).start()
+        own_second(k, h).start()
+        own_mate(k, h).start()
+
+    def spread_start(k, h):
+        spread_first(k, h).start()
+
+    def stage_two(k, h):
+        arrival(1, k, h, piece(from_tp(k), part, across_rep, h))
+        arrival(2, k, h, piece(from_tp(k), across_part, me, h))
+        corner(k, h).start()
+        first_mate(k, h).start()
+        second_mate(k, h).start()
+
+    def stage_three(k, h):
+        arrival(4, k, h, piece(from_tp(k), across_part, across_rep, h))
+        corner_mate(k, h).start()
+
+    def stage_end(k, h):
+        mate_rep = lax.rem(mate + 2, ranks)
+        arrival(3, k, h, piece(from_tp(k), part, mate, h))
+        arrival(5, k, h, piece(from_tp(k), part, mate_rep, h))
+        arrival(6, k, h, piece(from_tp(k), across_part, mate, h))
+        arrival(7, k, h, piece(from_tp(k), across_part, mate_rep, h))
+        for copy in (
+            spread_first, own_first, own_second, own_mate, corner, first_mate, second_mate, corner_mate,
+        ):
+            copy(k, h).wait_send()
+
+    def stage(body, j):
+        loop(*third[j // 2], lambda k: body(k, j % 2))
+
+    stage(spread_start, 0)
+    stage(spread_start, 1)
+
+    stage(spread_start, 2)
+    for i in range(2, steps):
+        pool_copy(i).start()
 
     def exact_columns(number, chosen, contract):
         high = jnp.floor(number * (1.0 / 64.0))
@@ -153,101 +246,14 @@
         ask_ref[d, :, :asked_width] = asking[d * TILE : (d + 1) * TILE]
         ask_ref[d, :, asked_width:] = asking_filled[d * TILE : (d + 1) * TILE]
 
-    pl.semaphore_wait(barrier, ranks + tp - 1)
-
     def ask(k):
         return remote(ask_ref.at[peer_rep(k)], asked_ref.at[me], ask_sem.at[0, k], ask_sem.at[1, k], rep=peer_rep(k))
 
     for k in range(1, ranks):
         ask(k).start()
-
-    mine = part * ranks + me
-
-    def piece(t, owner_part, owner_rep, h):
-        begin = pl.multiple_of((owner_part * ranks + owner_rep) * segment + h * half, half)
-        return weight_ref.at[t, pl.ds(begin, half)]
-
-    def hop(kind, k, h, spot_ref, **where):
-        return remote(spot_ref, spot_ref, weight_send.at[kind, 2 * k + h], weight_recv.at[kind, 2 * k + h], **where)
-
-    def spread_first(k, h):
-        other = peer_tp(k)
-        begin = pl.multiple_of(mine * segment + h * half, half)
-        columns = pl.ds(pl.multiple_of(other * local_width, 128), local_width)
-        return remote(
-            weight_hbm.at[pl.ds(begin, half), columns], piece(rank, part, me, h),
-            weight_send.at[0, 2 * k + h], weight_recv.at[0, 2 * k + h], tp=other,
-        )
-
-    def own_first(k, h):
-        return hop(1, k, h, piece(from_tp(k), part, me, h), rep=across_rep)
-
-    def own_second(k, h):
-        return hop(2, k, h, piece(from_tp(k), part, me, h), parts=across_part)
-
-    def own_mate(k, h):
-        return hop(3, k, h, piece(from_tp(k), part, me, h), rep=mate)
-
-    def corner(k, h):
-        if h == 0:
-            return hop(4, k, h, piece(from_tp(k), part, across_rep, h), parts=across_part)
-        return hop(4, k, h, piece(from_tp(k), across_part, me, h), rep=across_rep)
-
-    def first_mate(k, h):
-        return hop(5, k, h, piece(from_tp(k), part, across_rep, h), rep=mate)
-
-    def second_mate(k, h):
-        return hop(6, k, h, piece(from_tp(k), across_part, me, h), rep=mate)
-
-    def corner_mate(k, h):
-        return hop(7, k, h, piece(from_tp(k), across_part, across_rep, h), rep=mate)
-
-    def arrival(kind, k, h, spot_ref):
-        hop(kind, k, h, spot_ref, rep=mate).wait_recv()
-
-    def loop(low, high, body):
-        def run(k, _):
-            body(k)
-            return 0
-
-        lax.fori_loop(low, high, run, 0)
-
-    def stage_one(k, h):
-        arrival(0, k, h, piece(from_tp(k), part, me, h))
-        own_first(k, h).start()
-        own_second(k, h).start()
-        own_mate(k, h).start()
-
-    def stage_two(k, h):
-        arrival(1, k, h, piece(from_tp(k), part, across_rep, h))
-        arrival(2, k, h, piece(from_tp(k), across_part, me, h))
-        corner(k, h).start()
-        first_mate(k, h).start()
-        second_mate(k, h).start()
-
-    def stage_three(k, h):
-        arrival(4, k, h, piece(from_tp(k), across_part, across_rep, h))
-        corner_mate(k, h).start()
-
-    def stage_end(k, h):
-        mate_rep = lax.rem(mate + 2, ranks)
-        arrival(3, k, h, piece(from_tp(k), part, mate, h))
-        arrival(5, k, h, piece(from_tp(k), part, mate_rep, h))
-        arrival(6, k, h, piece(from_tp(k), across_part, mate, h))
-        arrival(7, k, h, piece(from_tp(k), across_part, mate_rep, h))
-        for copy in (
-            spread_first, own_first, own_second, own_mate, corner, first_mate, second_mate, corner_mate,
-        ):
-            copy(k, h).wait_send()
-
-    def stage(body, j):
-        loop(*third[j // 2], lambda k: body(k, j % 2))
-
-    stage(lambda k, h: spread_first(k, h).start(), 0)
-    stage(lambda k, h: spread_first(k, h).start(), 1)
-
-    for i in range(2, steps):
-        pool_copy(i).start()
+    stage(stage_one, 0)
+    stage(spread_start, 3)
+
     gains_ref[...] = gain_ref[...].astype(jnp.float32)
     own_columns = pl.ds(pl.multiple_of(rank * local_width, 128), local_width)
     own_weight = pltpu.make_async_copy(weight_hbm.at[:, own_columns], weight_ref.at[rank], local_sem.at[0])
@@ -333,6 +339,8 @@
             reply_ref.at[peer_rep(k)], replied_ref.at[me], reply_sem.at[0, k], reply_sem.at[1, k], rep=peer_rep(k)
         )
 
+    stage(stage_one, 1)
+    stage(spread_start, 4)
     middle = steps // 2
 
     def attend(step, _):
@@ -350,31 +358,34 @@
         token_owner = jnp.where(position < spread[1:2], spread[0:1], -1.0)
         row_id = lax.rem(iota((group * rows, 1), 0), rows).astype(jnp.float32)
         chunk = pl.ds(step * step_pages, step_pages)
+        ones = jnp.ones((tokens, width), jnp.bfloat16)
+        all_scores = []
         for c in range(copies):
             keys = pool_ref[chunk, c, 0].reshape(tokens, width)
+            all_scores.append(lax.dot_general(
+                query_ref[c], keys, (((1,), (1,)), ((), ())), preferred_element_type=jnp.float32
+            ))
+        for c in range(copies):
             values = pool_ref[chunk, c, 1].reshape(tokens, width)
-            scores = lax.dot_general(
-                query_ref[c], keys, (((1,), (1,)), ((), ())), preferred_element_type=jnp.float32
-            )
-            scores = jnp.where(token_owner == row_id, scores, NEVER)
-            before = top_ref[c, :, 0:1]
+            scores = jnp.where(token_owner == row_id, all_scores[c], NEVER)
+            before = top_ref[c]
             highest = jnp.maximum(before, jnp.max(scores, axis=1, keepdims=True))
             decay = jnp.exp2((before - highest) * factor)
-            weights = jnp.exp2((scores - highest) * factor)
-            mass = jnp.sum(weights, axis=1, keepdims=True)
-            context = jnp.dot(weights.astype(jnp.bfloat16), values, preferred_element_type=jnp.float32)
-            top_ref[c] = jnp.broadcast_to(highest, top_ref.shape[1:])
-            mass_ref[c] = mass_ref[c] * decay + mass
-            sum_ref[c] = sum_ref[c] * decay + context
-
-        for j in range(6):
-            if j >= 2:
-                pl.when(step == j - 1)(lambda j=j: stage(lambda k, h: spread_first(k, h).start(), j))
-            pl.when(step == j + 2)(lambda j=j: stage(stage_one, j))
-            if j + 4 < steps:
-                pl.when(step == j + 4)(lambda j=j: stage(stage_two, j))
-            if j + 6 < steps:
-                pl.when(step == j + 6)(lambda j=j: stage(stage_three, j))
+            weights = jnp.exp2((scores - highest[:, 0:1]) * factor).astype(jnp.bfloat16)
+            both = jnp.dot(weights, jnp.concatenate([values, ones], axis=1), preferred_element_type=jnp.float32)
+            top_ref[c] = highest
+            mass_ref[c] = mass_ref[c] * decay + both[:, width:]
+            sum_ref[c] = sum_ref[c] * decay + both[:, :width]
+
+        def at(when, body, j):
+            pl.when(step == when)(lambda: stage(body, j))
+
+        for when, body, j in (
+            (0, stage_one, 2), (0, spread_start, 5), (1, stage_two, 0), (2, stage_two, 1), (3, stage_one, 3),
+            (4, stage_three, 0), (5, stage_two, 2), (6, stage_one, 4), (7, stage_three, 1), (7, stage_two, 3),
+            (9, stage_one, 5), (9, stage_three, 2),
+        ):
+            at(when, body, j)
         return 0
 
     def pool_rest():
@@ -410,42 +421,51 @@
         )
 
     loop(1, tp, lambda k: gather(k).start())
-    for j in range(6):
-        if j + 4 >= steps:
-            stage(stage_two, j)
-    for j in range(6):
-        if j + 6 >= steps:
-            stage(stage_three, j)
-    for j in range(6):
-        stage(stage_end, j)
+    stage(stage_two, 4)
+    stage(stage_three, 3)
     own_weight.wait()
     load_residual.wait()
+    strip = next(n for n in (512, 384, 256, 128) if local_width % n == 0)
+    spans = [slice(begin, begin + strip) for begin in range(0, local_width, strip)]
+
+    def product(t, span):
+        return jnp.dot(gathered_ref[t], weight_ref[t, :, span], preferred_element_type=jnp.float32)
+
+    def products(j, span):
+        low, high = third[j]
+        total = out_ref[:, span]
+        if high - low == 1:
+            return total + product(from_tp(low), span)
+        return lax.fori_loop(low, high, lambda k, total: total + product(from_tp(k), span), total)
 
     def gathered(k):
         spot_ref = gathered_ref.at[from_tp(k)]
         remote(spot_ref, spot_ref, gather_sem.at[0, k], gather_sem.at[1, k], tp=from_tp(k)).wait_recv()
 
+    for span in spans:
+        out_ref[:, span] = residual_ref[:, span].astype(jnp.float32) + product(rank, span)
+    stage(stage_two, 5)
+    stage(stage_three, 4)
     loop(1, tp, gathered)
-
-    strip = next(n for n in (512, 384, 256, 128) if local_width % n == 0)
+    stage(stage_end, 0)
+    stage(stage_end, 1)
+    for span in spans:
+        out_ref[:, span] = products(0, span)
+    stage(stage_three, 5)
+    stage(stage_end, 2)
+    stage(stage_end, 3)
+    for span in spans:
+        out_ref[:, span] = products(1, span)
+    stage(stage_end, 4)
+    stage(stage_end, 5)
     square_sum = jnp.zeros((slots, 1), jnp.float32)
-    for begin in range(0, local_width, strip):
-        span = slice(begin, begin + strip)
-
-        def add(t, total):
-            return total + jnp.dot(gathered_ref[t], weight_ref[t, :, span], preferred_element_type=jnp.float32)
-
-        total = residual_ref[:, span].astype(jnp.float32)
-        if tp <= 4:
-            for t in range(tp):
-                total = add(t, total)
-        else:
-            total = lax.fori_loop(0, tp, add, total)
+    for span in spans:
+        total = products(2, span)
+        square_sum = square_sum + jnp.sum(total * total, axis=1, keepdims=True)
         for j in range(0, strip, 128):
-            tile = slice(begin + j, begin + j + 128)
-            gain = gains_ref[pl.ds((rank * local_width + begin + j) // 128, 1), :]
+            tile = slice(span.start + j, span.start + j + 128)
+            gain = gains_ref[pl.ds((rank * local_width + span.start + j) // 128, 1), :]
             out_ref[:, tile] = total[:, j : j + 128] * gain
-        square_sum = square_sum + jnp.sum(total * total, axis=1, keepdims=True)
     square_row = jnp.sum(jnp.where(diagonal, square_sum, 0.0), axis=0, keepdims=True)
     square_ref[...] = jnp.broadcast_to(square_row, square_ref.shape)
 
@@ -462,7 +482,9 @@
     loop(1, tp, shared)
     all_row = jnp.sum(squares_ref[...], axis=0)[0:1]
     all_column = jnp.sum(jnp.where(diagonal, all_row, 0.0), axis=1, keepdims=True)
-    scale_ref[...] = lax.rsqrt(all_column / (local_width * tp) + EPSILON)
+    scale = lax.rsqrt(all_column / (local_width * tp) + EPSILON)
+    for span in spans:
+        result_ref[:, span] = (out_ref[:, span] * scale).astype(result_ref.dtype)
     for k in range(1, ranks):
         ask(k).wait_send()
         reply(k).wait_send()
@@ -494,14 +516,13 @@
     scratch = lambda shape, kind: pltpu.VMEM(shape, kind)
     asked_width = (heads + 2 * copies) * width
     payload = asked_width + width
-    total, scale = pl.pallas_call(
+    return pl.pallas_call(
         functools.partial(layer_kernel, ranks, tp, copies, group, step_pages, factor),
         in_specs=[vmem] * 4 + [pl.BlockSpec(memory_space=pltpu.SMEM)] + [vmem] * 3 + [anywhere] * 3,
-        out_specs=[vmem] * 2,
-        out_shape=[
-            jax.ShapeDtypeStruct((slots, local_width), jnp.float32), jax.ShapeDtypeStruct((slots, 1), jnp.float32),
-        ],
+        out_specs=vmem,
+        out_shape=jax.ShapeDtypeStruct((slots, local_width), jnp.bfloat16),
         scratch_shapes=[
+            scratch((slots, local_width), jnp.float32),
             scratch(kv_pool.shape, jnp.bfloat16),
             scratch((tp, depth, local_width), jnp.bfloat16),
             scratch((slots, local_width), jnp.bfloat16),
@@ -538,7 +559,6 @@
         queries.reshape(-1, width), fresh_kv.reshape(-1, width), page_table.T, lengths[None, :], mig_src[0], mig_dst[0],
         mig_count, norm_gain.reshape(-1, 128), kv_pool, residual, out_weight,
     )
-    return (total * scale).astype(jnp.bfloat16)
 
 
 def solution(mesh):

time: 54.1 us -> 52.7 us (0.974)
  other arithmetic: 3.42 us -> 0 us
  local copies, waits for them, and re-layouts: 0 us -> 2.06 us
    convert_element_type x1 -> x0, other arithmetic: 2.47 us -> none  [on_device(): return (total * scale).astype(jnp.bfloat16)]
    unnamed x0 -> x1, local copies, waits for them, and re-layouts: none -> 2.06 us
    pallas_call x1 -> x0, other arithmetic: 0.94 us -> none  [on_device(): pl.pallas_call(functools.partial(layer_kernel, ranks, tp, copies, group,...]
where the time goes in v4:
time: 52.7 us; the launch traced here: 52.5 us
  Pallas kernels  50.4 us (96%)
  local copies, waits for them, and re-layouts  2.06 us (4%)
    pallas_call x1, Pallas kernels, on_device(): pl.pallas_call(functools.partial(layer_kernel, ranks, tp, copies, group,...  50.4 us
    unnamed x1, local copies, waits for them, and re-layouts  2.06 us

profile of v4, /device:TPU:0, one launch (start us, length us, event | category | flops | bytes accessed | tf_op | source)
XLA Modules:
  0.0 52.5 jit_solution(9633568865030603363)
XLA Ops:
  0.0 50.4 %shard_map.109 = bf16[128,3072]{1,0:T(8,128)(2,1)} custom-call(bf16[256,128]{1,0:T(8,128)(2,1)} %bitcast.8, bf16[512,128]{1,0:T(8,128)(2,1)} %bitcast.7, s32[8,128]{1,0:T(8,128)} %bitcast.10, s32[1,128]{1,0:T(1,128)} %bitcast.13, s32[4,32]{1,0:T(4,128)} %bitcast.11, s32[4,32]{1,0:T(4,128)} %bitcast.12, s32[1,4]{1,0:T(1,128)} %count_ref.1, ...), custom_call_target="tpu_custom_call" | custom-call | tf_op jit(solution)/shard_map/pallas_call | solution.py:519
  50.4 2.1 %copy.13 = bf16[128,3072]{1,0:T(8,128)(2,1)} copy(bf16[128,3072]{1,0:T(8,128)(2,1)} %shard_map.109) | data formatting | bytes 1572864
